TPU v7x, 512 devices: a whole 4x4x16 slice. The times are simulated.
512 devices in a mesh: dp: 4 (over z_lo), seq: 128 (over x, z_hi, y, core).
Axes of the slice: x: 4, y: 4, z: 16 (z_hi: 4, z_lo: 4; z = z_hi * 4 + z_lo), core: 2. Of those that a mesh axis runs over, the one named last changes fastest.
Arguments:
- tokens: bfloat16 [4, 32768, 2048], P('dp', 'seq'), may hold values from -6 to 6
- cotangent: bfloat16 [4, 32768, 2048], P('dp', 'seq'), may hold values from -6 to 6
- kernel: bfloat16 [32768, 2048], P('seq'), may hold values from -6 to 6
- first_factor: bfloat16 [128, 256, 256], P('seq'), may hold values from -0.375 to 0.375
- second_factor: bfloat16 [256, 128, 128], P('seq'), may hold values from -0.5 to 0.5
Outputs:
- grad_kernel: bfloat16 [32768, 2048], P('seq')
- grad_first: float32 [128, 256, 256], P('seq')
- grad_second: float32 [256, 128, 128], P('seq')
All inputs are finite; a program needn't handle non-finite values.
Results may differ from a plain program's by a relative error of at most 0.0058.
Values may be sent and summed in bfloat16 or wider, within the bound.
No kernel may reach another device: no remote copies, remote signals or barrier semaphores. Data moves between devices by JAX's collectives and lax.ppermute only.
A program may use at most 64 MiB of HBM per device.

v0:
```python
import math

import jax
import jax.numpy as jnp
from jax import lax
from jax.sharding import PartitionSpec as P


def shards(tokens, cotangent, kernel, first_factor, second_factor):
    local_rows = tokens.shape[1]
    channels = tokens.shape[2]
    column_blocks = second_factor.shape[0]
    mixed_in = jnp.einsum(
        "aqb,abc->aqc", first_factor, tokens, preferred_element_type=jnp.float32
    ).astype(jnp.bfloat16)
    mixed_up = jnp.einsum(
        "aqb,abc->aqc", first_factor, cotangent, preferred_element_type=jnp.float32
    ).astype(jnp.bfloat16)
    arrived_in = lax.all_to_all(mixed_in, "seq", split_axis=1, concat_axis=0, tiled=True)
    arrived_up = lax.all_to_all(mixed_up, "seq", split_axis=1, concat_axis=0, tiled=True)
    forward = jnp.einsum(
        "bpa,abc->bpc", second_factor, arrived_in, preferred_element_type=jnp.float32
    )
    backward = jnp.einsum(
        "bpa,abc->bpc", second_factor, arrived_up, preferred_element_type=jnp.float32
    )
    arrived_in, arrived_up, forward, backward = (arrived_in, arrived_up, forward, backward)
    kernel_local = kernel.reshape(column_blocks, -1, channels)
    kernel_grad = forward * backward
    weighted = (kernel_local * forward).astype(jnp.bfloat16)
    pulled = (kernel_local * backward).astype(jnp.bfloat16)
    second_grad = jnp.einsum(
        "bpc,abc->bpa", pulled, arrived_in, preferred_element_type=jnp.float32
    ) + jnp.einsum("bpc,abc->bpa", weighted, arrived_up, preferred_element_type=jnp.float32)
    spread = jnp.einsum(
        "bpa,bpc->abc", second_factor, weighted, preferred_element_type=jnp.float32
    ).astype(jnp.bfloat16)
    pulled_back = jnp.einsum(
        "bpa,bpc->abc", second_factor, pulled, preferred_element_type=jnp.float32
    ).astype(jnp.bfloat16)
    seq_share = 1.0 / math.sqrt(lax.axis_size("dp"))
    factor_share = 1.0 / math.sqrt(2.0 * channels * lax.axis_size("dp"))
    returned, returned_back = (
        lax.all_to_all(spread, "seq", split_axis=0, concat_axis=1, tiled=True),
        lax.all_to_all(pulled_back, "seq", split_axis=0, concat_axis=1, tiled=True),
    )
    first_grad = jnp.einsum(
        "aqc,abc->aqb", returned_back, tokens, preferred_element_type=jnp.float32
    ) + jnp.einsum("aqc,abc->aqb", returned, cotangent, preferred_element_type=jnp.float32)
    kernel_total, first_total, second_total = lax.psum((kernel_grad, first_grad, second_grad), "dp")
    kernel_out = (kernel_total * seq_share).astype(jnp.bfloat16)
    return (
        kernel_out.reshape(local_rows, channels),
        first_total * factor_share,
        second_total * factor_share,
    )


def solution(mesh):
    in_specs = (
        P("dp", "seq", None),
        P("dp", "seq", None),
        P("seq", None),
        P("seq", None, None),
        P("seq", None, None),
    )
    out_specs = (P("seq", None), P("seq", None, None), P("seq", None, None))
    return jax.shard_map(shards, mesh=mesh, in_specs=in_specs, out_specs=out_specs, check_vma=False)
```

profile of v0, /device:TPU:1, one launch (start us, length us, event | category | flops | bytes accessed | tf_op | source)
XLA Modules:
  0.0 452.6 jit_solution(16030501432791481532)
XLA Ops:
  7.2 0.0 copy-start
  7.2 1.2 copy-done
  8.4 1.3 fusion
  9.7 1.6 copy.66
  11.4 0.5 broadcast.2
  11.9 7.8 %reduce.5 = bf16[256,2048]{1,0:T(8,128)(2,1)} reduce(bf16[256,1,2048]{2,1,0:T(2,128)(2,1)S(1)} %bitcast.52, bf16[]{:T(256)} %broadcast.2), dimensions={1}, to_apply=%bitcast.51.reduce_sub_computation | reduce | bytes 2097154
  19.7 2.6 reshape.60
  22.3 23.9 %all-to-all-start = ((bf16[128,2,2048]{2,1,0:T(2,128)(2,1)}), bf16[128,2,2048]{2,1,0:T(2,128)(2,1)}, u32[]{:S(2)}, u32[]{:S(2)}) async-start(bf16[128,2,2048]{2,1,0:T(2,128)(2,1)} %reshape.60), calls=%async_computation | async-start | bytes 2097152 | tf_op jit(solution)/shard_map/all_to_all | solution.py:19
  46.2 0.4 fusion.1
  46.6 1.6 copy.65
  48.2 7.8 %reduce.4 = bf16[256,2048]{1,0:T(8,128)(2,1)} reduce(bf16[256,1,2048]{2,1,0:T(2,128)(2,1)S(1)} %bitcast.53, bf16[]{:T(256)} %broadcast.2), dimensions={1}, to_apply=%bitcast.50.reduce_sub_computation | reduce | bytes 2097154
  56.0 2.6 reshape.62
  58.6 40.9 %all-to-all-done = bf16[128,2,2048]{2,1,0:T(2,128)(2,1)} async-done(((bf16[128,2,2048]{2,1,0:T(2,128)(2,1)}), bf16[128,2,2048]{2,1,0:T(2,128)(2,1)}, u32[]{:S(2)}, u32[]{:S(2)}) %all-to-all-start) | async-done | bytes 1048608 | tf_op jit(solution)/shard_map/all_to_all | solution.py:19
  99.6 12.2 %all-to-all-start.1 = ((bf16[128,2,2048]{2,1,0:T(2,128)(2,1)}), bf16[128,2,2048]{2,1,0:T(2,128)(2,1)}, u32[]{:S(2)}, u32[]{:S(2)}) async-start(bf16[128,2,2048]{2,1,0:T(2,128)(2,1)} %reshape.62), calls=%async_computation.1 | async-start | bytes 2097152 | tf_op jit(solution)/shard_map/all_to_all | solution.py:20
  111.8 1.6 copy.41
  113.4 6.5 %reshape.61 = bf16[256,1,2048]{2,1,0:T(2,128)(2,1)S(1)} reshape(bf16[128,2,2048]{2,1,0:T(2,128)(2,1)} %all-to-all-done) | data formatting | bytes 2097152
  119.9 7.0 %bitcast_reduce_fusion.1 = bf16[256,2048]{1,0:T(8,128)(2,1)} fusion(bf16[256,1,2048]{2,1,0:T(2,128)(2,1)S(1)} %reshape.61), kind=kLoop, calls=%fused_computation.31 | loop fusion | bytes 2097152 | tf_op jit(solution)/shard_map/all_to_all | solution.py:19
  127.0 1.7 all_to_all.13
  128.7 23.2 %all-to-all-done.1 = bf16[128,2,2048]{2,1,0:T(2,128)(2,1)} async-done(((bf16[128,2,2048]{2,1,0:T(2,128)(2,1)}), bf16[128,2,2048]{2,1,0:T(2,128)(2,1)}, u32[]{:S(2)}, u32[]{:S(2)}) %all-to-all-start.1) | async-done | bytes 1048608 | tf_op jit(solution)/shard_map/all_to_all | solution.py:20
  151.9 7.6 %reshape.63 = bf16[256,1,2048]{2,1,0:T(2,128)(2,1)} reshape(bf16[128,2,2048]{2,1,0:T(2,128)(2,1)} %all-to-all-done.1) | data formatting | bytes 2097152
  159.6 0.0 copy-start.6
  159.6 8.7 %bitcast_reduce_fusion = bf16[256,2048]{1,0:T(8,128)(2,1)} fusion(bf16[256,1,2048]{2,1,0:T(2,128)(2,1)} %reshape.63), kind=kLoop, calls=%fused_computation.30 | loop fusion | bytes 2097152 | tf_op jit(solution)/shard_map/all_to_all | solution.py:20
  168.2 1.7 all_to_all.15
  170.0 0.7 convolution_bitcast_fusion
  170.7 0.9 copy-done.3
  171.6 2.6 multiply_convert_fusion
  174.2 1.0 copy-done.2
  175.2 1.4 fusion.2
  176.6 3.7 copy.42
  180.3 24.9 %all-to-all-start.2 = ((bf16[128,2,2048]{2,1,0:T(2,128)(2,1)}), bf16[128,2,2048]{2,1,0:T(2,128)(2,1)}, u32[]{:S(2)}, u32[]{:S(2)}) async-start(bf16[128,2,2048]{2,1,0:T(2,128)(2,1)} %copy.42), calls=%async_computation.2 | async-start | bytes 2097152 | tf_op jit(solution)/shard_map/all_to_all | solution.py:45
  205.3 2.6 fusion.3
  207.9 3.7 copy.44
  211.7 47.0 %all-to-all-done.2 = bf16[128,2,2048]{2,1,0:T(2,128)(2,1)} async-done(((bf16[128,2,2048]{2,1,0:T(2,128)(2,1)}), bf16[128,2,2048]{2,1,0:T(2,128)(2,1)}, u32[]{:S(2)}, u32[]{:S(2)}) %all-to-all-start.2) | async-done | bytes 1048608 | tf_op jit(solution)/shard_map/all_to_all | solution.py:45
  258.7 11.0 %all-to-all-start.3 = ((bf16[128,2,2048]{2,1,0:T(2,128)(2,1)}), bf16[128,2,2048]{2,1,0:T(2,128)(2,1)}, u32[]{:S(2)}, u32[]{:S(2)}) async-start(bf16[128,2,2048]{2,1,0:T(2,128)(2,1)} %copy.44), calls=%async_computation.3 | async-start | bytes 2097152 | tf_op jit(solution)/shard_map/all_to_all | solution.py:44
  269.7 0.0 all-reduce.3.cloned.1.call-start
  269.7 2.2 fusion.13
  271.9 1.6 convolution_add_fusion.1
  273.5 1.5 reshape.55
  275.0 0.5 fusion.7
  275.5 48.8 %all-to-all-done.3 = bf16[128,2,2048]{2,1,0:T(2,128)(2,1)} async-done(((bf16[128,2,2048]{2,1,0:T(2,128)(2,1)}), bf16[128,2,2048]{2,1,0:T(2,128)(2,1)}, u32[]{:S(2)}, u32[]{:S(2)}) %all-to-all-start.3) | async-done | bytes 1048608 | tf_op jit(solution)/shard_map/all_to_all | solution.py:44
  324.3 1.5 reshape.56
  325.7 1.2 fusion.4
  326.9 0.0 all-reduce.3.cloned.1.call-update
  326.9 114.1 %all-reduce.3.cloned.1.call-done = (f32[2,128,2048]{1,2,0:T(8,128)}, f32[1,256,256]{2,1,0:T(8,128)}, f32[2,128,128]{2,1,0:T(8,128)}) async-done(((f32[2,128,2048]{1,2,0:T(8,128)}, f32[1,256,256]{2,1,0:T(8,128)}, f32[2,128,128]{2,1,0:T(8,128)}), (f32[2,128,2048]{1,2,0:T(8,128)}, f32[1,256,256]{2,1,0:T(8,128)}, f32[2,128,128]{2,1,0:T(8,128)})) %all-reduce.3.cloned.1.call-update) | async-done | bytes 2490384 | tf_op jit(solution)/shard_map/psum | solution.py:50
  441.0 1.8 multiply_convert_fusion.2
  442.8 1.3 copy.40
  444.1 0.7 broadcast_multiply_fusion.1
  444.8 0.7 broadcast_multiply_fusion
  (17 shorter events, 0.0 us)
Async XLA Ops:
  7.2 1.2 copy-start
  19.6 26.5 %copy-start.4 = (bf16[1,256,2048]{2,1,0:T(8,128)(2,1)S(1)}, bf16[1,256,2048]{2,1,0:T(8,128)(2,1)}, u32[]{:S(2)}) copy-start(bf16[1,256,2048]{2,1,0:T(8,128)(2,1)} %param.6) | copy-start | bytes 3145732
  19.7 26.5 %copy-start.8 = (bf16[1,256,256]{2,1,0:T(8,128)(2,1)S(1)}, bf16[1,256,256]{2,1,0:T(8,128)(2,1)}, u32[]{:S(2)}) copy-start(bf16[1,256,256]{2,1,0:T(8,128)(2,1)} %param.8) | copy-start | bytes 393220
  22.3 77.3 %all-to-all-start = ((bf16[128,2,2048]{2,1,0:T(2,128)(2,1)}), bf16[128,2,2048]{2,1,0:T(2,128)(2,1)}, u32[]{:S(2)}, u32[]{:S(2)}) async-start(bf16[128,2,2048]{2,1,0:T(2,128)(2,1)} %reshape.60), calls=%async_computation | async-start | bytes 2097152 | tf_op jit(solution)/shard_map/all_to_all | solution.py:19
  56.0 55.8 %copy-start.7 = (bf16[256,2048]{1,0:T(8,128)(2,1)S(1)}, bf16[256,2048]{1,0:T(8,128)(2,1)}, u32[]{:S(2)}) copy-start(bf16[256,2048]{1,0:T(8,128)(2,1)} %param.7) | copy-start | bytes 3145732
  99.6 52.3 %all-to-all-start.1 = ((bf16[128,2,2048]{2,1,0:T(2,128)(2,1)}), bf16[128,2,2048]{2,1,0:T(2,128)(2,1)}, u32[]{:S(2)}, u32[]{:S(2)}) async-start(bf16[128,2,2048]{2,1,0:T(2,128)(2,1)} %reshape.62), calls=%async_computation.1 | async-start | bytes 2097152 | tf_op jit(solution)/shard_map/all_to_all | solution.py:20
  159.6 10.4 %copy-start.6 = (bf16[2,128,128]{2,1,0:T(8,128)(2,1)S(1)}, bf16[2,128,128]{2,1,0:T(8,128)(2,1)}, u32[]{:S(2)}) copy-start(bf16[2,128,128]{2,1,0:T(8,128)(2,1)} %param.9) | copy-start | bytes 196612
  170.0 1.6 copy-start.3
  174.2 1.0 copy-start.2
  180.3 78.3 %all-to-all-start.2 = ((bf16[128,2,2048]{2,1,0:T(2,128)(2,1)}), bf16[128,2,2048]{2,1,0:T(2,128)(2,1)}, u32[]{:S(2)}, u32[]{:S(2)}) async-start(bf16[128,2,2048]{2,1,0:T(2,128)(2,1)} %copy.42), calls=%async_computation.2 | async-start | bytes 2097152 | tf_op jit(solution)/shard_map/all_to_all | solution.py:45
  258.7 65.6 %all-to-all-start.3 = ((bf16[128,2,2048]{2,1,0:T(2,128)(2,1)}), bf16[128,2,2048]{2,1,0:T(2,128)(2,1)}, u32[]{:S(2)}, u32[]{:S(2)}) async-start(bf16[128,2,2048]{2,1,0:T(2,128)(2,1)} %copy.44), calls=%async_computation.3 | async-start | bytes 2097152 | tf_op jit(solution)/shard_map/all_to_all | solution.py:44
  269.7 171.3 %all-reduce.3.cloned.1.call-start = ((), (), s32[]{:S(2)}) async-start(), calls=%async_computation.4 | async-start | bytes 4980736 | tf_op jit(solution)/shard_map/psum | solution.py:50
  269.7 2.2 copy-start.1
  275.0 50.7 %copy-start.5 = (bf16[1,256,2048]{2,1,0:T(8,128)(2,1)S(1)}, bf16[1,256,2048]{2,1,0:T(8,128)(2,1)}, u32[]{:S(2)}) copy-start(bf16[1,256,2048]{2,1,0:T(8,128)(2,1)} %param.6) | copy-start | bytes 3145732
  441.0 3.1 copy-start.10
  441.0 3.8 copy-start.9
Sparse Core Ops, SparseCore 0:
  327.1 113.8 all-reduce.2
where the time goes:
time: 462 us; the launch traced here: 453 us
  waiting for transfers between devices  274 us (59%)
  starting transfers between devices  72.1 us (16%)
  local copies, waits for them, and re-layouts  58.8 us (13%)
  other arithmetic  18.7 us (4%)
  matrix products  14.5 us (3%)
  between operations  14.5 us (3%)
    psum x1, waiting for transfers between devices, shards(): lax.psum((kernel_grad, first_grad, second_grad), 'dp')  114 us
    all_to_all x1, waiting for transfers between devices, shards(): lax.all_to_all(spread, 'seq', split_axis=0, concat_axis=1, tiled=True)  48.8 us
    all_to_all x1, waiting for transfers between devices, shards(): lax.all_to_all(pulled_back, 'seq', split_axis=0, concat_axis=1, tiled=True)  47 us
    all_to_all x1, waiting for transfers between devices, shards(): lax.all_to_all(mixed_in, 'seq', split_axis=1, concat_axis=0, tiled=True)  40.9 us
    all_to_all x1, starting transfers between devices, shards(): lax.all_to_all(pulled_back, 'seq', split_axis=0, concat_axis=1, tiled=True)  24.9 us
    all_to_all x1, starting transfers between devices, shards(): lax.all_to_all(mixed_in, 'seq', split_axis=1, concat_axis=0, tiled=True)  23.9 us
    all_to_all x1, waiting for transfers between devices, shards(): lax.all_to_all(mixed_up, 'seq', split_axis=1, concat_axis=0, tiled=True)  23.2 us
    unnamed x27, local copies, waits for them, and re-layouts  23 us
  transfers between devices with their start and end apart: 5, of which 5 were waited for; matrix products, arithmetic and copies ran while one was open for 9% of the time, Pallas kernels for 0%

commit v1 on v0

v1 whole, which is shorter than its diff:
```python
import math

import jax
import jax.numpy as jnp
from jax import lax
from jax.experimental import pallas as pl
from jax.experimental.pallas import tpu as pltpu
from jax.sharding import PartitionSpec as P

LANES = 128


def nn(left, right):
    return lax.dot_general(left, right, (((1,), (0,)), ((), ())), preferred_element_type=jnp.float32)


def nt(left, right):
    return lax.dot_general(left, right, (((1,), (1,)), ((), ())), preferred_element_type=jnp.float32)


def tn(left, right):
    return lax.dot_general(left, right, (((0,), (0,)), ((), ())), preferred_element_type=jnp.float32)


def mix_kernel(own, cols, first_ref, tokens_ref, cotangent_ref, out_ref, rows_ref, factor_ref):
    groups, rows, _ = out_ref.shape

    @pl.when(pl.program_id(0) == 0)
    def _():
        for h in range(factor_ref.shape[0]):
            factor_ref[h] = first_ref[0, :, h * LANES : (h + 1) * LANES].astype(jnp.float32)

    for q in range(own):
        factor = jnp.concatenate(
            [
                factor_ref[h, pl.ds(q, groups, stride=own), :].astype(jnp.bfloat16)
                for h in range(factor_ref.shape[0])
            ],
            axis=1,
        )
        for t, ref in enumerate((tokens_ref, cotangent_ref)):
            mixed = nn(factor, ref[0])
            for ci in range(cols):
                rows_ref[pl.ds((t * cols + ci) * own + q, groups, stride=rows), :] = mixed[
                    :, ci * LANES : (ci + 1) * LANES
                ]
    out_ref[...] = rows_ref[...].reshape(groups, rows, LANES).astype(jnp.bfloat16)


def middle_kernel(
    own, cols, shares, arrived_ref, kernel_ref, second_ref, back_ref, kernel_out_ref, second_out_ref, rows_ref, total_ref
):
    _, groups, rows, _ = arrived_ref.shape
    step = pl.program_id(0)
    last = pl.num_programs(0) - 1
    seq_share, factor_share = shares

    @pl.when(step == 0)
    def _():
        total_ref[...] = jnp.zeros_like(total_ref)
        second_out_ref[...] = jnp.zeros_like(second_out_ref)

    rows_ref[...] = arrived_ref[0].astype(jnp.float32).reshape(groups * rows, LANES)
    for q in range(own):
        factor = second_ref[q]
        held = []
        for t in range(2):
            held.append(
                jnp.concatenate(
                    [
                        rows_ref[pl.ds((t * cols + ci) * own + q, groups, stride=rows), :].astype(jnp.bfloat16)
                        for ci in range(cols)
                    ],
                    axis=1,
                )
            )
        mixed_in, mixed_up = held
        forward = nn(factor, mixed_in)
        backward = nn(factor, mixed_up)
        points = factor.shape[0]
        scale = kernel_ref[q * points : (q + 1) * points, :].astype(jnp.float32)
        total_ref[q] += forward * backward
        weighted = (scale * forward).astype(jnp.bfloat16)
        pulled = (scale * backward).astype(jnp.bfloat16)
        second_out_ref[q] += (nt(pulled, mixed_in) + nt(weighted, mixed_up)) * factor_share
        for t, values in enumerate((weighted, pulled)):
            spread = tn(factor, values)
            for ci in range(cols):
                rows_ref[pl.ds((t * cols + ci) * own + q, groups, stride=rows), :] = spread[
                    :, ci * LANES : (ci + 1) * LANES
                ]
    back_ref[0] = rows_ref[...].reshape(groups, rows, LANES).astype(jnp.bfloat16)

    @pl.when(step == last)
    def _():
        own_points = total_ref.shape[0] * total_ref.shape[1]
        kernel_out_ref[...] = (total_ref[...] * seq_share).astype(jnp.bfloat16).reshape(own_points, -1)


def final_kernel(own, cols, factor_share, returned_ref, tokens_ref, cotangent_ref, out_ref, rows_ref, total_ref):
    groups, rows, _ = returned_ref.shape
    step = pl.program_id(0)
    last = pl.num_programs(0) - 1

    @pl.when(step == 0)
    def _():
        total_ref[...] = jnp.zeros_like(total_ref)

    rows_ref[...] = returned_ref[...].astype(jnp.float32).reshape(groups * rows, LANES)
    for q in range(own):
        held = []
        for t in range(2):
            held.append(
                jnp.concatenate(
                    [
                        rows_ref[pl.ds((t * cols + ci) * own + q, groups, stride=rows), :].astype(jnp.bfloat16)
                        for ci in range(cols)
                    ],
                    axis=1,
                )
            )
        spread, pulled_back = held
        part = nt(pulled_back, tokens_ref[0]) + nt(spread, cotangent_ref[0])
        for h in range(total_ref.shape[0]):
            total_ref[h, pl.ds(q, groups, stride=own), :] += part[:, h * LANES : (h + 1) * LANES]

    @pl.when(step == last)
    def _():
        for h in range(total_ref.shape[0]):
            out_ref[:, h * LANES : (h + 1) * LANES] = total_ref[h] * factor_share


def shards(tokens, cotangent, kernel, first_factor, second_factor):
    ranks, members = lax.axis_size("dp"), lax.axis_size("seq")
    _, local_rows, channels = tokens.shape
    own, points, _ = second_factor.shape
    share = channels // ranks
    cols = share // LANES
    rows = 2 * cols * own
    groups = local_rows // own
    seq_share = 1.0 / math.sqrt(ranks)
    factor_share = 1.0 / math.sqrt(2.0 * channels * ranks)
    both = pl.BlockSpec((1, local_rows, share), lambda k: (0, 0, k))
    message = jax.ShapeDtypeStruct((ranks * members, rows, LANES), jnp.bfloat16)
    params = pltpu.CompilerParams(dimension_semantics=("arbitrary",), vmem_limit_bytes=40 * 1024 * 1024)
    row_scratch = pltpu.VMEM((groups * rows, LANES), jnp.float32)

    with jax.named_scope("mix"):
        mixed = pl.pallas_call(
            lambda *refs: mix_kernel(own, cols, *refs),
            out_shape=message,
            grid=(ranks,),
            in_specs=[pl.BlockSpec((1, local_rows, local_rows), lambda k: (0, 0, 0)), both, both],
            out_specs=pl.BlockSpec((members, rows, LANES), lambda k: (k, 0, 0)),
            scratch_shapes=[row_scratch, pltpu.VMEM((local_rows // LANES, local_rows, LANES), jnp.float32)],
            compiler_params=params,
            name="mix",
        )(first_factor, tokens, cotangent)
    with jax.named_scope("send"):
        arrived = lax.all_to_all(mixed, ("dp", "seq"), split_axis=0, concat_axis=0, tiled=True)
    quarter = lax.dynamic_slice_in_dim(kernel, lax.axis_index("dp") * share, share, 1)
    with jax.named_scope("middle"):
        back, kernel_part, second_part = pl.pallas_call(
            lambda *refs: middle_kernel(own, cols, (seq_share, factor_share), *refs),
            out_shape=(
                jax.ShapeDtypeStruct((ranks, members, rows, LANES), jnp.bfloat16),
                jax.ShapeDtypeStruct((own * points, share), jnp.bfloat16),
                jax.ShapeDtypeStruct((own, points, members), jnp.float32),
            ),
            grid=(ranks,),
            in_specs=[
                pl.BlockSpec((1, members, rows, LANES), lambda s: (s, 0, 0, 0)),
                pl.BlockSpec((own * points, share), lambda s: (0, 0)),
                pl.BlockSpec((own, points, members), lambda s: (0, 0, 0)),
            ],
            out_specs=(
                pl.BlockSpec((1, members, rows, LANES), lambda s: (s, 0, 0, 0)),
                pl.BlockSpec((own * points, share), lambda s: (0, 0)),
                pl.BlockSpec((own, points, members), lambda s: (0, 0, 0)),
            ),
            scratch_shapes=[row_scratch, pltpu.VMEM((own, points, share), jnp.float32)],
            compiler_params=params,
            name="middle",
        )(arrived.reshape(ranks, members, rows, LANES), quarter, second_factor)
    with jax.named_scope("gather_kernel"):
        kernel_out = lax.all_gather(kernel_part, "dp", axis=1, tiled=True)
    with jax.named_scope("return"):
        returned = lax.all_to_all(
            back.reshape(ranks * members, rows, LANES), ("dp", "seq"), split_axis=0, concat_axis=0, tiled=True
        )
    with jax.named_scope("final"):
        first_part = pl.pallas_call(
            lambda *refs: final_kernel(own, cols, factor_share, *refs),
            out_shape=jax.ShapeDtypeStruct((local_rows, local_rows), jnp.float32),
            grid=(ranks,),
            in_specs=[pl.BlockSpec((members, rows, LANES), lambda k: (k, 0, 0)), both, both],
            out_specs=pl.BlockSpec((local_rows, local_rows), lambda k: (0, 0)),
            scratch_shapes=[row_scratch, pltpu.VMEM((local_rows // LANES, local_rows, LANES), jnp.float32)],
            compiler_params=params,
            name="final",
        )(returned, tokens, cotangent)
    with jax.named_scope("sum"):
        first_total, second_total = lax.psum((first_part, second_part), "dp")
    return kernel_out, first_total[None], second_total


def solution(mesh):
    in_specs = (
        P("dp", "seq", None),
        P("dp", "seq", None),
        P("seq", None),
        P("seq", None, None),
        P("seq", None, None),
    )
    out_specs = (P("seq", None), P("seq", None, None), P("seq", None, None))
    return jax.shard_map(shards, mesh=mesh, in_specs=in_specs, out_specs=out_specs, check_vma=False)
```

time: 462 us -> 343 us (0.74); the launches traced: 453 us -> 342 us
  local copies, waits for them, and re-layouts: 58.8 us -> 12.3 us
  starting transfers between devices: 72.1 us -> 35.4 us
  other arithmetic: 18.7 us -> 0 us
  matrix products: 14.5 us -> 0 us
  Pallas kernels: 0 us -> 10.7 us
  waiting for transfers between devices: 274 us -> 269 us
    psum x1, waiting for transfers between devices: 114 us -> 50 us  [shards(): first_total, second_total = lax.psum((first_part, second_part), 'dp')]
    all_to_all x4 -> x2, waiting for transfers between devices: 160 us -> 218 us  [the longest x1 117 us: shards(): lax.all_to_all(back.reshape(ranks * members, rows, LANES), ('dp', 'seq'),...]
    all_to_all x4 -> x2, starting transfers between devices: 72 us -> 35.3 us  [the longest x1 24.3 us: shards(): lax.all_to_all(mixed, ('dp', 'seq'), split_axis=0, concat_axis=0, tiled=T...]
    all_to_all x4 -> x0, local copies, waits for them, and re-layouts: 19.2 us -> none  [the longest x2 10.4 us: shards(): lax.all_to_all(mixed_up, 'seq', split_axis=1, concat_axis=0, tiled=True)]
    unnamed x2 -> x0, other arithmetic: 15.5 us -> none
    dot_general x10 -> x0, matrix products: 14.5 us -> none  [the longest x1 2.65 us: shards(): jnp.einsum('bpa,bpc->abc', second_factor, weighted, preferred_element_typ...]
    convert_element_type x6 -> x0, local copies, waits for them, and re-layouts: 13.6 us -> none  [the longest x1 3.73 us: shards(): spread = jnp.einsum('bpa,bpc->abc', second_factor, weighted, preferred_el...]
    unnamed x27 -> x25, local copies, waits for them, and re-layouts: 23 us -> 12.3 us
  transfers between devices with their start and end apart: 5 -> 4, of which waited for: 5 -> 3; matrix products, arithmetic and copies ran while one was open for 9% -> 0% of each run, Pallas kernels for 0% -> 1%
where the time goes in v1:
time: 343 us; the launch traced here: 342 us
  waiting for transfers between devices  269 us (78%)
  starting transfers between devices  35.4 us (10%)
  between operations  14.1 us (4%)
  local copies, waits for them, and re-layouts  12.3 us (4%)
  Pallas kernels  10.7 us (3%)
    all_to_all x1, waiting for transfers between devices, shards(): lax.all_to_all(back.reshape(ranks * members, rows, LANES), ('dp', 'seq'),...  117 us
    all_to_all x1, waiting for transfers between devices, shards(): lax.all_to_all(mixed, ('dp', 'seq'), split_axis=0, concat_axis=0, tiled=T...  101 us
    psum x1, waiting for transfers between devices, shards(): first_total, second_total = lax.psum((first_part, second_part), 'dp')  50 us
    all_to_all x1, starting transfers between devices, shards(): lax.all_to_all(mixed, ('dp', 'seq'), split_axis=0, concat_axis=0, tiled=T...  24.3 us
    unnamed x25, local copies, waits for them, and re-layouts  12.3 us
    all_to_all x1, starting transfers between devices, shards(): lax.all_to_all(back.reshape(ranks * members, rows, LANES), ('dp', 'seq'),...  11 us
  transfers between devices with their start and end apart: 4, of which 3 were waited for; matrix products, arithmetic and copies ran while one was open for 0% of the time, Pallas kernels for 1%

profile of v1, /device:TPU:1, one launch (start us, length us, event | category | flops | bytes accessed | tf_op | source)
XLA Modules:
  0.0 341.6 jit_solution(15770906798076669986)
XLA Ops:
  7.2 0.0 copy-start
  7.2 0.0 copy-start.2
  7.2 1.3 copy-done.2
  8.5 0.0 copy-start.4
  8.5 1.2 copy-done.4
  9.7 0.0 copy-start.7
  9.7 0.9 copy-done.7
  10.6 2.4 mix.1
  13.0 0.0 copy-start.1
  13.0 1.3 copy-done.1
  14.4 0.0 copy-start.8
  14.4 24.3 %all-to-all-start = ((bf16[512,16,128]{2,1,0:T(8,128)(2,1)}), bf16[512,16,128]{2,1,0:T(8,128)(2,1)S(1)}, u32[]{:S(2)}, u32[]{:S(2)}) async-start(bf16[512,16,128]{2,1,0:T(8,128)(2,1)} %copy-done.1), calls=%async_computation | async-start | bytes 4194304 | tf_op jit(solution)/shard_map/send/all_to_all | solution.py:160
  38.7 0.0 copy-done
  38.7 101.1 %all-to-all-done = bf16[512,16,128]{2,1,0:T(8,128)(2,1)S(1)} async-done(((bf16[512,16,128]{2,1,0:T(8,128)(2,1)}), bf16[512,16,128]{2,1,0:T(8,128)(2,1)S(1)}, u32[]{:S(2)}, u32[]{:S(2)}) %all-to-all-start) | async-done | bytes 2097184 | tf_op jit(solution)/shard_map/send/all_to_all | solution.py:160
  139.8 0.0 copy-done.8
  139.8 5.3 %middle.1 = (bf16[4,128,16,128]{3,2,1,0:T(8,128)(2,1)S(1)}, bf16[256,512]{1,0:T(8,128)(2,1)}, f32[2,128,128]{2,1,0:T(8,128)}) custom-call(bf16[4,128,16,128]{3,2,1,0:T(8,128)(2,1)S(1)} %bitcast.3, bf16[256,512]{1,0:T(8,128)(2,1)S(1)} %constant_dynamic-slice_fusion.refs_1_, bf16[2,128,128]{2,1,0:T(8,128)(2,1)S(1)} %copy-done.8), custom_call_target="tpu_custom_call" | custom-call | tf_op jit(solution)/shard_map/middle/middle/pallas_call | solution.py:163
  145.1 0.0 copy-start.6
  145.1 1.3 copy-done.6
  146.5 11.0 %all-to-all-start.1 = ((bf16[512,16,128]{2,1,0:T(8,128)(2,1)}), bf16[512,16,128]{2,1,0:T(8,128)(2,1)S(1)}, u32[]{:S(2)}, u32[]{:S(2)}) async-start(bf16[512,16,128]{2,1,0:T(8,128)(2,1)} %bitcast.4), calls=%async_computation.1 | async-start | bytes 4194304 | tf_op jit(solution)/shard_map/return/all_to_all | solution.py:188
  157.5 0.0 all-gather.2.cloned.1.call-start
  157.5 0.7 all-gather.2.cloned.1.call-update
  158.2 0.0 all-reduce.3.cloned.1.call-start
  158.3 117.3 %all-to-all-done.1.refs_0_ = bf16[512,16,128]{2,1,0:T(8,128)(2,1)S(1)} async-done(((bf16[512,16,128]{2,1,0:T(8,128)(2,1)}), bf16[512,16,128]{2,1,0:T(8,128)(2,1)S(1)}, u32[]{:S(2)}, u32[]{:S(2)}) %all-to-all-start.1) | async-done | bytes 2097184 | tf_op jit(solution)/shard_map/return/all_to_all | solution.py:188
  275.6 0.0 copy-start.3
  275.6 1.2 copy-done.3
  276.8 0.0 copy-start.5
  276.8 1.2 copy-done.5
  278.1 3.0 final.1
  281.0 0.0 all-reduce.3.cloned.1.call-update
  281.1 0.0 all-gather.2.cloned.1.call-done
  281.1 50.0 %all-reduce.3.cloned.1.call-done = (f32[1,256,256]{2,1,0:T(8,128)}, f32[2,128,128]{2,1,0:T(8,128)}) async-done(((f32[1,256,256]{2,1,0:T(8,128)}, f32[2,128,128]{2,1,0:T(8,128)}), (f32[1,256,256]{2,1,0:T(8,128)}, f32[2,128,128]{2,1,0:T(8,128)})) %all-reduce.3.cloned.1.call-update) | async-done | bytes 393232 | tf_op jit(solution)/shard_map/sum/psum | solution.py:203
  331.1 0.0 copy-start.9
  331.1 0.0 copy-start.10
  331.1 2.4 copy.11
  333.4 0.0 copy-done.9
  333.4 0.7 copy.12
  334.1 0.0 copy-done.10
  334.1 0.7 copy.13
  (1 shorter events, 0.0 us)
Async XLA Ops:
  7.2 31.5 %copy-start = (bf16[256,2048]{1,0:T(8,128)(2,1)S(1)}, bf16[256,2048]{1,0:T(8,128)(2,1)}, u32[]{:S(2)}) copy-start(bf16[256,2048]{1,0:T(8,128)(2,1)} %param.7) | copy-start | bytes 3145732
  7.2 1.3 copy-start.2
  8.5 1.2 copy-start.4
  9.7 0.9 copy-start.7
  13.0 1.3 copy-start.1
  14.4 125.4 %copy-start.8 = (bf16[2,128,128]{2,1,0:T(8,128)(2,1)S(1)}, bf16[2,128,128]{2,1,0:T(8,128)(2,1)}, u32[]{:S(2)}) copy-start(bf16[2,128,128]{2,1,0:T(8,128)(2,1)} %refs_2_.4) | copy-start | bytes 196612
  14.4 125.4 %all-to-all-start = ((bf16[512,16,128]{2,1,0:T(8,128)(2,1)}), bf16[512,16,128]{2,1,0:T(8,128)(2,1)S(1)}, u32[]{:S(2)}, u32[]{:S(2)}) async-start(bf16[512,16,128]{2,1,0:T(8,128)(2,1)} %copy-done.1), calls=%async_computation | async-start | bytes 4194304 | tf_op jit(solution)/shard_map/send/all_to_all | solution.py:160
  145.1 1.3 copy-start.6
  146.5 129.1 %all-to-all-start.1 = ((bf16[512,16,128]{2,1,0:T(8,128)(2,1)}), bf16[512,16,128]{2,1,0:T(8,128)(2,1)S(1)}, u32[]{:S(2)}, u32[]{:S(2)}) async-start(bf16[512,16,128]{2,1,0:T(8,128)(2,1)} %bitcast.4), calls=%async_computation.1 | async-start | bytes 4194304 | tf_op jit(solution)/shard_map/return/all_to_all | solution.py:188
  157.5 123.6 %all-gather.2.cloned.1.call-start = ((), (), s32[]{:S(2)}) async-start(), calls=%async_computation.2 | async-start | bytes 1310720 | tf_op jit(solution)/shard_map/gather_kernel/all_gather | solution.py:186
  158.2 172.8 %all-reduce.3.cloned.1.call-start = ((), (), s32[]{:S(2)}) async-start(), calls=%async_computation.3 | async-start | bytes 786432 | tf_op jit(solution)/shard_map/sum/psum | solution.py:203
  275.6 1.2 copy-start.3
  276.8 1.2 copy-start.5
  331.1 2.4 copy-start.9
  331.1 3.1 copy-start.10
Sparse Core Ops, SparseCore 0:
  161.0 102.5 all-gather.1
  281.2 49.8 all-reduce.2

commit v2 on v1

--- a/solution.py
+++ b/solution.py
@@ -47,8 +47,19 @@
     out_ref[...] = rows_ref[...].reshape(groups, rows, LANES).astype(jnp.bfloat16)
 
 
+def pack(blocks_ref, part_ref, start):
+    own, points, _ = blocks_ref.shape
+    fold = part_ref.shape[1] // LANES
+    height = points // fold
+    for q in range(own):
+        for f in range(fold):
+            part_ref[start + q * height : start + (q + 1) * height, f * LANES : (f + 1) * LANES] = blocks_ref[
+                q, f * height : (f + 1) * height, :
+            ].astype(jnp.bfloat16)
+
+
 def middle_kernel(
-    own, cols, shares, arrived_ref, kernel_ref, second_ref, back_ref, kernel_out_ref, second_out_ref, rows_ref, total_ref
+    own, cols, shares, arrived_ref, kernel_ref, second_ref, back_ref, part_ref, rows_ref, total_ref, second_ref_total
 ):
     _, groups, rows, _ = arrived_ref.shape
     step = pl.program_id(0)
@@ -58,7 +69,7 @@
     @pl.when(step == 0)
     def _():
         total_ref[...] = jnp.zeros_like(total_ref)
-        second_out_ref[...] = jnp.zeros_like(second_out_ref)
+        second_ref_total[...] = jnp.zeros_like(second_ref_total)
 
     rows_ref[...] = arrived_ref[0].astype(jnp.float32).reshape(groups * rows, LANES)
     for q in range(own):
@@ -82,7 +93,7 @@
         total_ref[q] += forward * backward
         weighted = (scale * forward).astype(jnp.bfloat16)
         pulled = (scale * backward).astype(jnp.bfloat16)
-        second_out_ref[q] += (nt(pulled, mixed_in) + nt(weighted, mixed_up)) * factor_share
+        second_ref_total[q] += (nt(pulled, mixed_in) + nt(weighted, mixed_up)) * factor_share
         for t, values in enumerate((weighted, pulled)):
             spread = tn(factor, values)
             for ci in range(cols):
@@ -93,20 +104,37 @@
 
     @pl.when(step == last)
     def _():
-        own_points = total_ref.shape[0] * total_ref.shape[1]
-        kernel_out_ref[...] = (total_ref[...] * seq_share).astype(jnp.bfloat16).reshape(own_points, -1)
-
-
-def final_kernel(own, cols, factor_share, returned_ref, tokens_ref, cotangent_ref, out_ref, rows_ref, total_ref):
+        points = total_ref.shape[1]
+        for q in range(own):
+            part_ref[q * points : (q + 1) * points, :] = (total_ref[q] * seq_share).astype(jnp.bfloat16)
+        pack(second_ref_total, part_ref, own * points)
+
+
+def final_kernel(
+    own, cols, ranks, factor_share, returned_ref, tokens_ref, cotangent_ref, out_ref, rows_ref, total_ref, held_ref, sems
+):
     groups, rows, _ = returned_ref.shape
+    share = cols * LANES
     step = pl.program_id(0)
     last = pl.num_programs(0) - 1
 
+    def loads(k):
+        chunk = pl.ds(pl.multiple_of(k * share, share), share)
+        return [
+            pltpu.make_async_copy(ref.at[0, :, chunk], held_ref.at[t, k], sems.at[t, k])
+            for t, ref in enumerate((tokens_ref, cotangent_ref))
+        ]
+
     @pl.when(step == 0)
     def _():
+        for k in range(ranks):
+            for copy in loads(k):
+                copy.start()
         total_ref[...] = jnp.zeros_like(total_ref)
 
     rows_ref[...] = returned_ref[...].astype(jnp.float32).reshape(groups * rows, LANES)
+    for copy in loads(step):
+        copy.wait()
     for q in range(own):
         held = []
         for t in range(2):
@@ -120,14 +148,43 @@
                 )
             )
         spread, pulled_back = held
-        part = nt(pulled_back, tokens_ref[0]) + nt(spread, cotangent_ref[0])
+        part = nt(pulled_back, held_ref[0, step]) + nt(spread, held_ref[1, step])
         for h in range(total_ref.shape[0]):
             total_ref[h, pl.ds(q, groups, stride=own), :] += part[:, h * LANES : (h + 1) * LANES]
 
     @pl.when(step == last)
     def _():
         for h in range(total_ref.shape[0]):
-            out_ref[:, h * LANES : (h + 1) * LANES] = total_ref[h] * factor_share
+            out_ref[:, h * LANES : (h + 1) * LANES] = (total_ref[h] * factor_share).astype(jnp.bfloat16)
+
+
+def join_kernel(ranks, *refs):
+    firsts_ref, pieces, outs = refs[0], refs[1 : 1 + ranks], refs[1 + ranks :]
+    kernel_out_ref, first_out_ref, second_out_ref = outs
+    own, points, _ = second_out_ref.shape
+    share = pieces[0].shape[1]
+    me = lax.axis_index("dp")
+    for r in range(ranks):
+        chunk = pl.ds(pl.multiple_of(lax.rem(me + ranks - r, ranks) * share, share), share)
+        kernel_out_ref[:, chunk] = pieces[r][: own * points, :]
+    first = firsts_ref[0].astype(jnp.float32)
+    for k in range(1, ranks):
+        first += firsts_ref[k].astype(jnp.float32)
+    first_out_ref[...] = first
+    total = None
+    for j in range(ranks):
+        piece = pieces[0][own * points :, :]
+        for r in range(1, ranks):
+            piece = jnp.where(lax.rem(j + r, ranks) == me, pieces[r][own * points :, :], piece)
+        piece = piece.astype(jnp.float32)
+        total = piece if total is None else total + piece
+    fold = share // LANES
+    height = points // fold
+    for q in range(own):
+        for f in range(fold):
+            second_out_ref[q, f * height : (f + 1) * height, :] = total[
+                q * height : (q + 1) * height, f * LANES : (f + 1) * LANES
+            ]
 
 
 def shards(tokens, cotangent, kernel, first_factor, second_factor):
@@ -138,11 +195,13 @@
     cols = share // LANES
     rows = 2 * cols * own
     groups = local_rows // own
+    second_rows = own * points * members // share
     seq_share = 1.0 / math.sqrt(ranks)
     factor_share = 1.0 / math.sqrt(2.0 * channels * ranks)
     both = pl.BlockSpec((1, local_rows, share), lambda k: (0, 0, k))
     message = jax.ShapeDtypeStruct((ranks * members, rows, LANES), jnp.bfloat16)
-    params = pltpu.CompilerParams(dimension_semantics=("arbitrary",), vmem_limit_bytes=40 * 1024 * 1024)
+    params = pltpu.CompilerParams(dimension_semantics=("arbitrary",), vmem_limit_bytes=32 * 1024 * 1024)
+    wide = pltpu.CompilerParams(dimension_semantics=("arbitrary",), vmem_limit_bytes=58 * 1024 * 1024)
     row_scratch = pltpu.VMEM((groups * rows, LANES), jnp.float32)
 
     with jax.named_scope("mix"):
@@ -153,19 +212,18 @@
             in_specs=[pl.BlockSpec((1, local_rows, local_rows), lambda k: (0, 0, 0)), both, both],
             out_specs=pl.BlockSpec((members, rows, LANES), lambda k: (k, 0, 0)),
             scratch_shapes=[row_scratch, pltpu.VMEM((local_rows // LANES, local_rows, LANES), jnp.float32)],
-            compiler_params=params,
+            compiler_params=wide,
             name="mix",
         )(first_factor, tokens, cotangent)
     with jax.named_scope("send"):
         arrived = lax.all_to_all(mixed, ("dp", "seq"), split_axis=0, concat_axis=0, tiled=True)
     quarter = lax.dynamic_slice_in_dim(kernel, lax.axis_index("dp") * share, share, 1)
     with jax.named_scope("middle"):
-        back, kernel_part, second_part = pl.pallas_call(
+        back, part = pl.pallas_call(
             lambda *refs: middle_kernel(own, cols, (seq_share, factor_share), *refs),
             out_shape=(
                 jax.ShapeDtypeStruct((ranks, members, rows, LANES), jnp.bfloat16),
-                jax.ShapeDtypeStruct((own * points, share), jnp.bfloat16),
-                jax.ShapeDtypeStruct((own, points, members), jnp.float32),
+                jax.ShapeDtypeStruct((own * points + second_rows, share), jnp.bfloat16),
             ),
             grid=(ranks,),
             in_specs=[
@@ -175,33 +233,56 @@
             ],
             out_specs=(
                 pl.BlockSpec((1, members, rows, LANES), lambda s: (s, 0, 0, 0)),
-                pl.BlockSpec((own * points, share), lambda s: (0, 0)),
-                pl.BlockSpec((own, points, members), lambda s: (0, 0, 0)),
-            ),
-            scratch_shapes=[row_scratch, pltpu.VMEM((own, points, share), jnp.float32)],
+                pl.BlockSpec((own * points + second_rows, share), lambda s: (0, 0)),
+            ),
+            scratch_shapes=[
+                row_scratch,
+                pltpu.VMEM((own, points, share), jnp.float32),
+                pltpu.VMEM((own, points, members), jnp.float32),
+            ],
             compiler_params=params,
             name="middle",
         )(arrived.reshape(ranks, members, rows, LANES), quarter, second_factor)
-    with jax.named_scope("gather_kernel"):
-        kernel_out = lax.all_gather(kernel_part, "dp", axis=1, tiled=True)
+    with jax.named_scope("gather_parts"):
+        pieces = [part]
+        for r in range(1, ranks):
+            pieces.append(lax.ppermute(part, "dp", [(i, (i + r) % ranks) for i in range(ranks)]))
     with jax.named_scope("return"):
         returned = lax.all_to_all(
             back.reshape(ranks * members, rows, LANES), ("dp", "seq"), split_axis=0, concat_axis=0, tiled=True
         )
     with jax.named_scope("final"):
+        whole = pl.BlockSpec(memory_space=pl.ANY)
         first_part = pl.pallas_call(
-            lambda *refs: final_kernel(own, cols, factor_share, *refs),
-            out_shape=jax.ShapeDtypeStruct((local_rows, local_rows), jnp.float32),
+            lambda *refs: final_kernel(own, cols, ranks, factor_share, *refs),
+            out_shape=jax.ShapeDtypeStruct((local_rows, local_rows), jnp.bfloat16),
             grid=(ranks,),
-            in_specs=[pl.BlockSpec((members, rows, LANES), lambda k: (k, 0, 0)), both, both],
+            in_specs=[pl.BlockSpec((members, rows, LANES), lambda k: (k, 0, 0)), whole, whole],
             out_specs=pl.BlockSpec((local_rows, local_rows), lambda k: (0, 0)),
-            scratch_shapes=[row_scratch, pltpu.VMEM((local_rows // LANES, local_rows, LANES), jnp.float32)],
-            compiler_params=params,
+            scratch_shapes=[
+                row_scratch,
+                pltpu.VMEM((local_rows // LANES, local_rows, LANES), jnp.float32),
+                pltpu.VMEM((2, ranks, local_rows, share), jnp.bfloat16),
+                pltpu.SemaphoreType.DMA((2, ranks)),
+            ],
+            compiler_params=pltpu.CompilerParams(
+                dimension_semantics=("arbitrary",), vmem_limit_bytes=58 * 1024 * 1024
+            ),
             name="final",
         )(returned, tokens, cotangent)
     with jax.named_scope("sum"):
-        first_total, second_total = lax.psum((first_part, second_part), "dp")
-    return kernel_out, first_total[None], second_total
+        first_parts = lax.all_gather(first_part, "dp")
+        kernel_out, first_out, second_out = pl.pallas_call(
+            lambda *refs: join_kernel(ranks, *refs),
+            out_shape=(
+                jax.ShapeDtypeStruct((own * points, channels), jnp.bfloat16),
+                jax.ShapeDtypeStruct((local_rows, local_rows), jnp.float32),
+                jax.ShapeDtypeStruct((own, points, members), jnp.float32),
+            ),
+            compiler_params=pltpu.CompilerParams(vmem_limit_bytes=32 * 1024 * 1024),
+            name="join",
+        )(first_parts, *pieces)
+    return kernel_out, first_out[None], second_out
 
 
 def solution(mesh):

time: 343 us -> 282 us (0.82)
  waiting for transfers between devices: 269 us -> 190 us
  blocking collectives: 0 us -> 22.7 us
  between operations: 14.1 us -> 0.75 us
  starting transfers between devices: 35.4 us -> 48.1 us
  local copies, waits for them, and re-layouts: 12.3 us -> 2.07 us
  Pallas kernels: 10.7 us -> 16.4 us
    psum x1 -> x0, waiting for transfers between devices: 50 us -> none  [shards(): first_total, second_total = lax.psum((first_part, second_part), 'dp')]
    all_to_all x1, waiting for transfers between devices: 117 us -> 88.9 us  [shards(): lax.all_to_all(back.reshape(ranks * members, rows, LANES), ('dp', 'seq'),...]
    all_gather x0 -> x1, blocking collectives: none -> 22.7 us  [shards(): first_parts = lax.all_gather(first_part, 'dp')]
    unnamed x25 -> x10, local copies, waits for them, and re-layouts: 12.3 us -> 2.04 us
    ppermute x0 -> x3, starting transfers between devices: none -> 10 us  [shards(): lax.ppermute(part, 'dp', [(i, (i + r) % ranks) for i in range(ranks)])]
    pallas_call x1 -> x2, Pallas kernels: 2.97 us -> 6.82 us  [the longest x1 5.61 us: shards(): pl.pallas_call(lambda *refs: final_kernel(own, cols, ranks, factor_share,...]
  transfers between devices with their start and end apart: 4 -> 5, of which waited for: 3 -> 2; matrix products, arithmetic and copies ran while one was open for 0% -> 0% of each run, Pallas kernels for 1% -> 2%
where the time goes in v2:
time: 282 us; the launch traced here: 280 us
  waiting for transfers between devices  190 us (67%)
  starting transfers between devices  48.1 us (17%)
  blocking collectives  22.7 us (8%)
  Pallas kernels  16.4 us (6%)
    all_to_all x1, waiting for transfers between devices, shards(): lax.all_to_all(mixed, ('dp', 'seq'), split_axis=0, concat_axis=0, tiled=T...  101 us
    all_to_all x1, waiting for transfers between devices, shards(): lax.all_to_all(back.reshape(ranks * members, rows, LANES), ('dp', 'seq'),...  88.9 us
    all_to_all x1, starting transfers between devices, shards(): lax.all_to_all(mixed, ('dp', 'seq'), split_axis=0, concat_axis=0, tiled=T...  24.3 us
    all_gather x1, blocking collectives, shards(): first_parts = lax.all_gather(first_part, 'dp')  22.7 us
    all_to_all x1, starting transfers between devices, shards(): lax.all_to_all(back.reshape(ranks * members, rows, LANES), ('dp', 'seq'),...  13.8 us
    ppermute x3, starting transfers between devices, shards(): lax.ppermute(part, 'dp', [(i, (i + r) % ranks) for i in range(ranks)])  10 us
  transfers between devices with their start and end apart: 5, of which 2 were waited for; matrix products, arithmetic and copies ran while one was open for 0% of the time, Pallas kernels for 2%

profile of v2, /device:TPU:1, one launch (start us, length us, event | category | flops | bytes accessed | tf_op | source)
XLA Modules:
  0.0 280.0 jit_solution(12023577152255819316)
XLA Ops:
  0.6 0.0 copy-start
  0.6 4.9 %mix.1 = bf16[512,16,128]{2,1,0:T(8,128)(2,1)} custom-call(bf16[1,256,256]{2,1,0:T(8,128)(2,1)} %refs_0_.1, bf16[1,256,2048]{2,1,0:T(8,128)(2,1)} %refs_1_.3, bf16[1,256,2048]{2,1,0:T(8,128)(2,1)} %refs_2_.5), custom_call_target="tpu_custom_call" | custom-call | tf_op jit(solution)/shard_map/mix/mix/pallas_call | solution.py:208
  5.6 0.0 copy-start.4
  5.6 24.3 %all-to-all-start = ((bf16[512,16,128]{2,1,0:T(8,128)(2,1)}), bf16[512,16,128]{2,1,0:T(8,128)(2,1)S(1)}, u32[]{:S(2)}, u32[]{:S(2)}) async-start(bf16[512,16,128]{2,1,0:T(8,128)(2,1)} %mix.1), calls=%async_computation | async-start | bytes 4194304 | tf_op jit(solution)/shard_map/send/all_to_all | solution.py:219
  29.9 0.0 copy-done
  29.9 101.1 %all-to-all-done = bf16[512,16,128]{2,1,0:T(8,128)(2,1)S(1)} async-done(((bf16[512,16,128]{2,1,0:T(8,128)(2,1)}), bf16[512,16,128]{2,1,0:T(8,128)(2,1)S(1)}, u32[]{:S(2)}, u32[]{:S(2)}) %all-to-all-start) | async-done | bytes 2097184 | tf_op jit(solution)/shard_map/send/all_to_all | solution.py:219
  131.0 0.0 copy-done.4
  131.0 4.6 %middle.1 = (bf16[4,128,16,128]{3,2,1,0:T(8,128)(2,1)S(1)}, bf16[320,512]{1,0:T(8,128)(2,1)S(1)}) custom-call(bf16[4,128,16,128]{3,2,1,0:T(8,128)(2,1)S(1)} %bitcast.4, bf16[256,512]{1,0:T(8,128)(2,1)S(1)} %constant_dynamic-slice_fusion.refs_1_, bf16[2,128,128]{2,1,0:T(8,128)(2,1)S(1)} %copy-done.4), custom_call_target="tpu_custom_call" | custom-call | tf_op jit(solution)/shard_map/middle/middle/pallas_call | solution.py:222
  135.6 0.0 copy-start.1
  135.6 1.3 copy-done.1
  136.9 0.0 copy-start.2
  136.9 0.7 copy-done.2
  137.6 0.0 copy-start.3
  137.6 13.8 %all-to-all-start.1 = ((bf16[512,16,128]{2,1,0:T(8,128)(2,1)}), bf16[512,16,128]{2,1,0:T(8,128)(2,1)}, u32[]{:S(2)}, u32[]{:S(2)}) async-start(bf16[512,16,128]{2,1,0:T(8,128)(2,1)} %bitcast.6), calls=%async_computation.1 | async-start | bytes 4194304 | tf_op jit(solution)/shard_map/return/all_to_all | solution.py:251
  151.5 0.0 copy-done.3
  151.5 5.9 %collective-permute-start.2 = (bf16[320,512]{1,0:T(8,128)(2,1)S(1)}, bf16[320,512]{1,0:T(8,128)(2,1)S(1)}, u32[]{:S(2)}, u32[]{:S(2)}) collective-permute-start(bf16[320,512]{1,0:T(8,128)(2,1)S(1)} %copy-done.3), channel_id=1, source_target_pairs={{0,384},{128,0},{256,128},{384,256},{1,385},{129,1},{257,129},{385... | collective-permute-start | bytes 983048 | tf_op jit(solution)/shard_map/gather_parts/ppermute | solution.py:249
  157.4 1.9 collective-permute-start.1
  159.3 2.2 collective-permute-start
  161.5 88.9 %all-to-all-done.1.refs_0_ = bf16[512,16,128]{2,1,0:T(8,128)(2,1)} async-done(((bf16[512,16,128]{2,1,0:T(8,128)(2,1)}), bf16[512,16,128]{2,1,0:T(8,128)(2,1)}, u32[]{:S(2)}, u32[]{:S(2)}) %all-to-all-start.1) | async-done | bytes 2097184 | tf_op jit(solution)/shard_map/return/all_to_all | solution.py:251
  250.4 5.6 %final.1 = bf16[256,256]{1,0:T(8,128)(2,1)} custom-call(bf16[512,16,128]{2,1,0:T(8,128)(2,1)} %all-to-all-done.1.refs_0_, bf16[1,256,2048]{2,1,0:T(8,128)(2,1)} %refs_1_.3, bf16[1,256,2048]{2,1,0:T(8,128)(2,1)} %refs_2_.5), custom_call_target="tpu_custom_call" | custom-call | tf_op jit(solution)/shard_map/final/final/pallas_call | solution.py:256
  256.0 22.7 %all-gather = bf16[1024,256]{1,0:T(8,128)(2,1)S(1)} all-gather(bf16[256,256]{1,0:T(8,128)(2,1)} %final.1), channel_id=2, replica_groups=mesh['dp'=4,'seq'=128] {'dp'}, dimensions={0}, use_global_device_ids=true | all-gather | bytes 655360 | tf_op jit(solution)/shard_map/sum/all_gather | solution.py:274
  278.8 0.0 collective-permute-done.2.refs_4_
  278.8 0.0 collective-permute-done.1.refs_3_
  278.8 0.0 collective-permute-done.refs_2_
  278.8 1.2 join.1
  (1 shorter events, 0.0 us)
Async XLA Ops:
  0.6 29.3 %copy-start = (bf16[256,2048]{1,0:T(8,128)(2,1)S(1)}, bf16[256,2048]{1,0:T(8,128)(2,1)}, u32[]{:S(2)}) copy-start(bf16[256,2048]{1,0:T(8,128)(2,1)} %param.7) | copy-start | bytes 3145732
  5.6 125.4 %copy-start.4 = (bf16[2,128,128]{2,1,0:T(8,128)(2,1)S(1)}, bf16[2,128,128]{2,1,0:T(8,128)(2,1)}, u32[]{:S(2)}) copy-start(bf16[2,128,128]{2,1,0:T(8,128)(2,1)} %refs_2_.4) | copy-start | bytes 196612
  5.6 125.4 %all-to-all-start = ((bf16[512,16,128]{2,1,0:T(8,128)(2,1)}), bf16[512,16,128]{2,1,0:T(8,128)(2,1)S(1)}, u32[]{:S(2)}, u32[]{:S(2)}) async-start(bf16[512,16,128]{2,1,0:T(8,128)(2,1)} %mix.1), calls=%async_computation | async-start | bytes 4194304 | tf_op jit(solution)/shard_map/send/all_to_all | solution.py:219
  135.6 1.3 copy-start.1
  136.9 0.7 copy-start.2
  137.6 13.8 %copy-start.3 = (bf16[320,512]{1,0:T(8,128)(2,1)S(1)}, bf16[320,512]{1,0:T(8,128)(2,1)}, u32[]{:S(2)}) copy-start(bf16[320,512]{1,0:T(8,128)(2,1)} %copy-done.2) | copy-start | bytes 983044
  137.6 112.8 %all-to-all-start.1 = ((bf16[512,16,128]{2,1,0:T(8,128)(2,1)}), bf16[512,16,128]{2,1,0:T(8,128)(2,1)}, u32[]{:S(2)}, u32[]{:S(2)}) async-start(bf16[512,16,128]{2,1,0:T(8,128)(2,1)} %bitcast.6), calls=%async_computation.1 | async-start | bytes 4194304 | tf_op jit(solution)/shard_map/return/all_to_all | solution.py:251
  151.5 127.3 %collective-permute-start.2 = (bf16[320,512]{1,0:T(8,128)(2,1)S(1)}, bf16[320,512]{1,0:T(8,128)(2,1)S(1)}, u32[]{:S(2)}, u32[]{:S(2)}) collective-permute-start(bf16[320,512]{1,0:T(8,128)(2,1)S(1)} %copy-done.3), channel_id=1, source_target_pairs={{0,384},{128,0},{256,128},{384,256},{1,385},{129,1},{257,129},{385... | collective-permute-start | bytes 983048 | tf_op jit(solution)/shard_map/gather_parts/ppermute | solution.py:249
  157.4 121.4 %collective-permute-start.1 = (bf16[320,512]{1,0:T(8,128)(2,1)S(1)}, bf16[320,512]{1,0:T(8,128)(2,1)S(1)}, u32[]{:S(2)}, u32[]{:S(2)}) collective-permute-start(bf16[320,512]{1,0:T(8,128)(2,1)S(1)} %copy-done.3), channel_id=1, source_target_pairs={{0,256},{128,384},{256,0},{384,128},{1,257},{129,385},{257,1},{385... | collective-permute-start | bytes 983048 | tf_op jit(solution)/shard_map/gather_parts/ppermute | solution.py:249
  159.3 119.4 %collective-permute-start = (bf16[320,512]{1,0:T(8,128)(2,1)S(1)}, bf16[320,512]{1,0:T(8,128)(2,1)S(1)}, u32[]{:S(2)}, u32[]{:S(2)}) collective-permute-start(bf16[320,512]{1,0:T(8,128)(2,1)S(1)} %copy-done.3), channel_id=1, source_target_pairs={{0,128},{128,256},{256,384},{384,0},{1,129},{129,257},{257,385},{3... | collective-permute-start | bytes 983048 | tf_op jit(solution)/shard_map/gather_parts/ppermute | solution.py:249

commit v3 on v2

v3 whole, which is shorter than its diff:
```python
import math

import jax
import jax.numpy as jnp
from jax import lax
from jax.experimental import pallas as pl
from jax.experimental.pallas import tpu as pltpu
from jax.sharding import PartitionSpec as P

LANES = 128


def nn(left, right):
    return lax.dot_general(left, right, (((1,), (0,)), ((), ())), preferred_element_type=jnp.float32)


def nt(left, right):
    return lax.dot_general(left, right, (((1,), (1,)), ((), ())), preferred_element_type=jnp.float32)


def tn(left, right):
    return lax.dot_general(left, right, (((0,), (0,)), ((), ())), preferred_element_type=jnp.float32)


def beside(rows, own, cols, q):
    return [
        jnp.concatenate([rows[(t * cols + ci) * own + q] for ci in range(cols)], axis=1) for t in range(2)
    ]


def mix_kernel(own, cols, first_ref, tokens_ref, cotangent_ref, out_ref, factor_ref):
    groups = out_ref.shape[0]

    @pl.when(pl.program_id(0) == 0)
    def _():
        for h in range(factor_ref.shape[0]):
            factor_ref[h] = first_ref[0, :, h * LANES : (h + 1) * LANES].astype(jnp.float32)

    pieces = [None] * out_ref.shape[1]
    for q in range(own):
        factor = jnp.concatenate(
            [
                factor_ref[h, pl.ds(q, groups, stride=own), :].astype(jnp.bfloat16)
                for h in range(factor_ref.shape[0])
            ],
            axis=1,
        )
        for t, ref in enumerate((tokens_ref, cotangent_ref)):
            mixed = nn(factor, ref[0]).astype(jnp.bfloat16)
            for ci in range(cols):
                pieces[(t * cols + ci) * own + q] = mixed[:, ci * LANES : (ci + 1) * LANES]
    out_ref[...] = jnp.swapaxes(jnp.stack(pieces), 0, 1)


def pack(blocks_ref, part_ref, start):
    own, points, _ = blocks_ref.shape
    fold = part_ref.shape[1] // LANES
    height = points // fold
    for q in range(own):
        for f in range(fold):
            part_ref[start + q * height : start + (q + 1) * height, f * LANES : (f + 1) * LANES] = blocks_ref[
                q, f * height : (f + 1) * height, :
            ].astype(jnp.bfloat16)


def middle_kernel(
    own, cols, shares, arrived_ref, kernel_ref, second_ref, back_ref, part_ref, total_ref, second_total_ref
):
    step = pl.program_id(0)
    last = pl.num_programs(0) - 1
    seq_share, factor_share = shares

    @pl.when(step == 0)
    def _():
        total_ref[...] = jnp.zeros_like(total_ref)
        second_total_ref[...] = jnp.zeros_like(second_total_ref)

    arrived = jnp.swapaxes(arrived_ref[0], 0, 1)
    pieces = [None] * arrived.shape[0]
    for q in range(own):
        factor = second_ref[q]
        mixed_in, mixed_up = beside(arrived, own, cols, q)
        forward = nn(factor, mixed_in)
        backward = nn(factor, mixed_up)
        points = factor.shape[0]
        scale = kernel_ref[q * points : (q + 1) * points, :].astype(jnp.float32)
        total_ref[q] += forward * backward
        weighted = (scale * forward).astype(jnp.bfloat16)
        pulled = (scale * backward).astype(jnp.bfloat16)
        second_total_ref[q] += (nt(pulled, mixed_in) + nt(weighted, mixed_up)) * factor_share
        for t, values in enumerate((weighted, pulled)):
            spread = tn(factor, values).astype(jnp.bfloat16)
            for ci in range(cols):
                pieces[(t * cols + ci) * own + q] = spread[:, ci * LANES : (ci + 1) * LANES]
    back_ref[0] = jnp.swapaxes(jnp.stack(pieces), 0, 1)

    @pl.when(step == last)
    def _():
        points = total_ref.shape[1]
        for q in range(own):
            part_ref[q * points : (q + 1) * points, :] = (total_ref[q] * seq_share).astype(jnp.bfloat16)
        pack(second_total_ref, part_ref, own * points)


def final_kernel(
    own, cols, ranks, factor_share, returned_ref, tokens_ref, cotangent_ref, out_ref, total_ref, rows_ref, held_ref, sems
):
    groups = returned_ref.shape[0]
    share = cols * LANES
    step = pl.program_id(0)
    last = pl.num_programs(0) - 1

    def loads(k):
        chunk = pl.ds(pl.multiple_of(k * share, share), share)
        return [
            pltpu.make_async_copy(ref.at[0, :, chunk], held_ref.at[t, k], sems.at[t, k])
            for t, ref in enumerate((tokens_ref, cotangent_ref))
        ]

    @pl.when(step == 0)
    def _():
        for k in range(ranks):
            for copy in loads(k):
                copy.start()
        total_ref[...] = jnp.zeros_like(total_ref)

    returned = jnp.swapaxes(returned_ref[...], 0, 1)
    for copy in loads(step):
        copy.wait()
    for q in range(own):
        spread, pulled_back = beside(returned, own, cols, q)
        total_ref[q] += nt(pulled_back, held_ref[0, step]) + nt(spread, held_ref[1, step])

    @pl.when(step == last)
    def _():
        for h in range(rows_ref.shape[0]):
            for q in range(own):
                rows_ref[h, pl.ds(q, groups, stride=own), :] = total_ref[q, :, h * LANES : (h + 1) * LANES]
            out_ref[:, h * LANES : (h + 1) * LANES] = (rows_ref[h] * factor_share).astype(jnp.bfloat16)


def join_kernel(ranks, firsts_ref, *refs):
    pieces, refs = refs[:ranks], refs[ranks:]
    kernel_out_ref, first_out_ref, second_out_ref, tails_ref, sems = refs
    own, points, _ = second_out_ref.shape
    _, tail_rows, share = tails_ref.shape
    me = lax.axis_index("dp")
    copies = []
    for r in range(ranks):
        sender = lax.rem(me + ranks - r, ranks)
        chunk = pl.ds(pl.multiple_of(sender * share, share), share)
        copies.append(
            (
                pltpu.make_async_copy(
                    pieces[r].at[pl.ds(0, own * points), :], kernel_out_ref.at[:, chunk], sems.at[0, r]
                ),
                pltpu.make_async_copy(
                    pieces[r].at[pl.ds(own * points, tail_rows), :], tails_ref.at[sender], sems.at[1, r]
                ),
            )
        )
    for pair in copies:
        for copy in pair:
            copy.start()
    first = firsts_ref[0].astype(jnp.float32)
    for k in range(1, ranks):
        first += firsts_ref[k].astype(jnp.float32)
    first_out_ref[...] = first
    for pair in copies:
        pair[1].wait()
    total = tails_ref[0].astype(jnp.float32)
    for k in range(1, ranks):
        total += tails_ref[k].astype(jnp.float32)
    fold = share // LANES
    height = points // fold
    for q in range(own):
        for f in range(fold):
            second_out_ref[q, f * height : (f + 1) * height, :] = total[
                q * height : (q + 1) * height, f * LANES : (f + 1) * LANES
            ]
    for pair in copies:
        pair[0].wait()


def in_hbm(array):
    return pltpu.with_memory_space_constraint(array, pltpu.HBM)


def shards(tokens, cotangent, kernel, first_factor, second_factor):
    ranks, members = lax.axis_size("dp"), lax.axis_size("seq")
    _, local_rows, channels = tokens.shape
    own, points, _ = second_factor.shape
    share = channels // ranks
    cols = share // LANES
    rows = 2 * cols * own
    groups = local_rows // own
    second_rows = own * points * members // share
    seq_share = 1.0 / math.sqrt(ranks)
    factor_share = 1.0 / math.sqrt(2.0 * channels * ranks)
    both = pl.BlockSpec((1, local_rows, share), lambda k: (0, 0, k))
    params = pltpu.CompilerParams(dimension_semantics=("arbitrary",), vmem_limit_bytes=32 * 1024 * 1024)

    with jax.named_scope("mix"):
        mixed = pl.pallas_call(
            lambda *refs: mix_kernel(own, cols, *refs),
            out_shape=pltpu.HBM((ranks * members, rows, LANES), jnp.bfloat16),
            grid=(ranks,),
            in_specs=[pl.BlockSpec((1, local_rows, local_rows), lambda k: (0, 0, 0)), both, both],
            out_specs=pl.BlockSpec((members, rows, LANES), lambda k: (k, 0, 0)),
            scratch_shapes=[pltpu.VMEM((local_rows // LANES, local_rows, LANES), jnp.float32)],
            compiler_params=params,
            name="mix",
        )(in_hbm(first_factor), in_hbm(tokens), in_hbm(cotangent))
    with jax.named_scope("send"):
        arrived = lax.all_to_all(mixed, ("dp", "seq"), split_axis=0, concat_axis=0, tiled=True)
    quarter = lax.dynamic_slice_in_dim(kernel, lax.axis_index("dp") * share, share, 1)
    with jax.named_scope("middle"):
        back, part = pl.pallas_call(
            lambda *refs: middle_kernel(own, cols, (seq_share, factor_share), *refs),
            out_shape=(
                pltpu.HBM((ranks, members, rows, LANES), jnp.bfloat16),
                pltpu.HBM((own * points + second_rows, share), jnp.bfloat16),
            ),
            grid=(ranks,),
            in_specs=[
                pl.BlockSpec((1, members, rows, LANES), lambda s: (s, 0, 0, 0)),
                pl.BlockSpec((own * points, share), lambda s: (0, 0)),
                pl.BlockSpec((own, points, members), lambda s: (0, 0, 0)),
            ],
            out_specs=(
                pl.BlockSpec((1, members, rows, LANES), lambda s: (s, 0, 0, 0)),
                pl.BlockSpec((own * points + second_rows, share), lambda s: (0, 0)),
            ),
            scratch_shapes=[
                pltpu.VMEM((own, points, share), jnp.float32),
                pltpu.VMEM((own, points, members), jnp.float32),
            ],
            compiler_params=params,
            name="middle",
        )(arrived.reshape(ranks, members, rows, LANES), quarter, second_factor)
    with jax.named_scope("gather_parts"):
        pieces = [part]
        for r in range(1, ranks):
            pieces.append(lax.ppermute(part, "dp", [(i, (i + r) % ranks) for i in range(ranks)]))
    with jax.named_scope("return"):
        returned = lax.all_to_all(
            back.reshape(ranks * members, rows, LANES), ("dp", "seq"), split_axis=0, concat_axis=0, tiled=True
        )
    with jax.named_scope("final"):
        whole = pl.BlockSpec(memory_space=pl.ANY)
        first_part = pl.pallas_call(
            lambda *refs: final_kernel(own, cols, ranks, factor_share, *refs),
            out_shape=jax.ShapeDtypeStruct((local_rows, local_rows), jnp.bfloat16),
            grid=(ranks,),
            in_specs=[pl.BlockSpec((members, rows, LANES), lambda k: (k, 0, 0)), whole, whole],
            out_specs=pl.BlockSpec((local_rows, local_rows), lambda k: (0, 0)),
            scratch_shapes=[
                pltpu.VMEM((own, groups, local_rows), jnp.float32),
                pltpu.VMEM((local_rows // LANES, local_rows, LANES), jnp.float32),
                pltpu.VMEM((2, ranks, local_rows, share), jnp.bfloat16),
                pltpu.SemaphoreType.DMA((2, ranks)),
            ],
            compiler_params=params,
            name="final",
        )(returned, in_hbm(tokens), in_hbm(cotangent))
    with jax.named_scope("sum"):
        first_parts = lax.all_gather(first_part, "dp")
        kernel_out, first_out, second_out = pl.pallas_call(
            lambda *refs: join_kernel(ranks, *refs),
            out_shape=(
                jax.ShapeDtypeStruct((own * points, channels), jnp.bfloat16),
                jax.ShapeDtypeStruct((local_rows, local_rows), jnp.float32),
                jax.ShapeDtypeStruct((own, points, members), jnp.float32),
            ),
            in_specs=[pl.BlockSpec(memory_space=pltpu.VMEM)] + [whole] * ranks,
            out_specs=(
                whole,
                pl.BlockSpec(memory_space=pltpu.VMEM),
                pl.BlockSpec(memory_space=pltpu.VMEM),
            ),
            scratch_shapes=[
                pltpu.VMEM((ranks, second_rows, share), jnp.bfloat16),
                pltpu.SemaphoreType.DMA((2, ranks)),
            ],
            compiler_params=pltpu.CompilerParams(vmem_limit_bytes=32 * 1024 * 1024),
            name="join",
        )(first_parts, *pieces)
    return kernel_out, first_out[None], second_out


def solution(mesh):
    in_specs = (
        P("dp", "seq", None),
        P("dp", "seq", None),
        P("seq", None),
        P("seq", None, None),
        P("seq", None, None),
    )
    out_specs = (P("seq", None), P("seq", None, None), P("seq", None, None))
    return jax.shard_map(shards, mesh=mesh, in_specs=in_specs, out_specs=out_specs, check_vma=False)
```

time: 282 us -> 303 us (1.074)
  Pallas kernels: 16.4 us -> 38.3 us
    pallas_call x1, Pallas kernels: 1.21 us -> 25.8 us  [shards(): pl.pallas_call(lambda *refs: join_kernel(ranks, *refs), out_shape=(jax.Sh...]
  transfers between devices with their start and end apart: 5 -> 5, of which waited for: 2 -> 2; matrix products, arithmetic and copies ran while one was open for 0% -> 0% of each run, Pallas kernels for 2% -> 1%
where the time goes in v3:
time: 303 us; the launch traced here: 301 us
  waiting for transfers between devices  192 us (63%)
  starting transfers between devices  45.5 us (15%)
  Pallas kernels  38.3 us (13%)
  blocking collectives  25 us (8%)
    all_to_all x1, waiting for transfers between devices, shards(): lax.all_to_all(mixed, ('dp', 'seq'), split_axis=0, concat_axis=0, tiled=T...  101 us
    all_to_all x1, waiting for transfers between devices, shards(): lax.all_to_all(back.reshape(ranks * members, rows, LANES), ('dp', 'seq'),...  90.8 us
    pallas_call x1, Pallas kernels, shards(): pl.pallas_call(lambda *refs: join_kernel(ranks, *refs), out_shape=(jax.Sh...  25.8 us
    all_gather x1, blocking collectives, shards(): first_parts = lax.all_gather(first_part, 'dp')  25 us
    all_to_all x1, starting transfers between devices, shards(): lax.all_to_all(mixed, ('dp', 'seq'), split_axis=0, concat_axis=0, tiled=T...  24.3 us
    all_to_all x1, starting transfers between devices, shards(): lax.all_to_all(back.reshape(ranks * members, rows, LANES), ('dp', 'seq'),...  11.2 us
    ppermute x3, starting transfers between devices, shards(): lax.ppermute(part, 'dp', [(i, (i + r) % ranks) for i in range(ranks)])  10 us
  transfers between devices with their start and end apart: 5, of which 2 were waited for; matrix products, arithmetic and copies ran while one was open for 0% of the time, Pallas kernels for 1%

profile of v3, /device:TPU:1, one launch (start us, length us, event | category | flops | bytes accessed | tf_op | source)
XLA Modules:
  0.0 301.4 jit_solution(17406690853569171641)
XLA Ops:
  0.6 0.0 copy-start
  0.6 4.5 %mix.1 = bf16[512,16,128]{2,1,0:T(8,128)(2,1)} custom-call(bf16[1,256,256]{2,1,0:T(8,128)(2,1)} %refs_0_.1, bf16[1,256,2048]{2,1,0:T(8,128)(2,1)} %refs_1_.3, bf16[1,256,2048]{2,1,0:T(8,128)(2,1)} %refs_2_.5), custom_call_target="tpu_custom_call" | custom-call | tf_op jit(solution)/shard_map/mix/mix/pallas_call | solution.py:204
  5.2 0.0 copy-start.2
  5.2 24.3 %all-to-all-start = ((bf16[512,16,128]{2,1,0:T(8,128)(2,1)}), bf16[512,16,128]{2,1,0:T(8,128)(2,1)S(1)}, u32[]{:S(2)}, u32[]{:S(2)}) async-start(bf16[512,16,128]{2,1,0:T(8,128)(2,1)} %mix.1), calls=%async_computation | async-start | bytes 4194304 | tf_op jit(solution)/shard_map/send/all_to_all | solution.py:215
  29.5 0.0 copy-done
  29.5 101.1 %all-to-all-done = bf16[512,16,128]{2,1,0:T(8,128)(2,1)S(1)} async-done(((bf16[512,16,128]{2,1,0:T(8,128)(2,1)}), bf16[512,16,128]{2,1,0:T(8,128)(2,1)S(1)}, u32[]{:S(2)}, u32[]{:S(2)}) %all-to-all-start) | async-done | bytes 2097184 | tf_op jit(solution)/shard_map/send/all_to_all | solution.py:215
  130.6 0.0 copy-done.2
  130.6 4.5 %middle.1 = (bf16[4,128,16,128]{3,2,1,0:T(8,128)(2,1)}, bf16[320,512]{1,0:T(8,128)(2,1)}) custom-call(bf16[4,128,16,128]{3,2,1,0:T(8,128)(2,1)S(1)} %bitcast.4, bf16[256,512]{1,0:T(8,128)(2,1)S(1)} %constant_dynamic-slice_fusion.refs_1_, bf16[2,128,128]{2,1,0:T(8,128)(2,1)S(1)} %copy-done.2), custom_call_target="tpu_custom_call" | custom-call | tf_op jit(solution)/shard_map/middle/middle/pallas_call | solution.py:218
  135.0 0.0 copy-start.1
  135.1 11.2 %all-to-all-start.1 = ((bf16[512,16,128]{2,1,0:T(8,128)(2,1)}), bf16[512,16,128]{2,1,0:T(8,128)(2,1)S(1)}, u32[]{:S(2)}, u32[]{:S(2)}) async-start(bf16[512,16,128]{2,1,0:T(8,128)(2,1)} %bitcast.6), calls=%async_computation.1 | async-start | bytes 4194304 | tf_op jit(solution)/shard_map/return/all_to_all | solution.py:246
  146.2 0.0 copy-done.1
  146.2 5.9 %collective-permute-start.2 = (bf16[320,512]{1,0:T(8,128)(2,1)S(1)}, bf16[320,512]{1,0:T(8,128)(2,1)}, u32[]{:S(2)}, u32[]{:S(2)}) collective-permute-start(bf16[320,512]{1,0:T(8,128)(2,1)S(1)} %copy-done.1), channel_id=1, source_target_pairs={{0,384},{128,0},{256,128},{384,256},{1,385},{129,1},{257,129},{385... | collective-permute-start | bytes 983048 | tf_op jit(solution)/shard_map/gather_parts/ppermute | solution.py:244
  152.1 1.9 collective-permute-start.1
  154.1 2.2 collective-permute-start
  156.3 90.8 %all-to-all-done.1.refs_0_ = bf16[512,16,128]{2,1,0:T(8,128)(2,1)S(1)} async-done(((bf16[512,16,128]{2,1,0:T(8,128)(2,1)}), bf16[512,16,128]{2,1,0:T(8,128)(2,1)S(1)}, u32[]{:S(2)}, u32[]{:S(2)}) %all-to-all-start.1) | async-done | bytes 2097184 | tf_op jit(solution)/shard_map/return/all_to_all | solution.py:246
  247.1 3.5 %final.1 = bf16[256,256]{1,0:T(8,128)(2,1)S(1)} custom-call(bf16[512,16,128]{2,1,0:T(8,128)(2,1)S(1)} %all-to-all-done.1.refs_0_, bf16[1,256,2048]{2,1,0:T(8,128)(2,1)} %refs_1_.3, bf16[1,256,2048]{2,1,0:T(8,128)(2,1)} %refs_2_.5), custom_call_target="tpu_custom_call" | custom-call | tf_op jit(solution)/shard_map/final/final/pallas_call | solution.py:251
  250.6 25.0 %all-gather = bf16[1024,256]{1,0:T(8,128)(2,1)S(1)} all-gather(bf16[256,256]{1,0:T(8,128)(2,1)S(1)} %final.1), channel_id=2, replica_groups=mesh['dp'=4,'seq'=128] {'dp'}, dimensions={0}, use_global_device_ids=true | all-gather | bytes 655360 | tf_op jit(solution)/shard_map/sum/all_gather | solution.py:267
  275.6 0.0 collective-permute-done.2.refs_4_
  275.6 0.0 collective-permute-done.1.refs_3_
  275.6 0.0 collective-permute-done.refs_2_
  275.6 25.8 %join.1 = (bf16[256,2048]{1,0:T(8,128)(2,1)}, f32[256,256]{1,0:T(8,128)}, f32[2,128,128]{2,1,0:T(8,128)}) custom-call(bf16[4,256,256]{2,1,0:T(8,128)(2,1)S(1)} %bitcast.5, bf16[320,512]{1,0:T(8,128)(2,1)S(1)} %copy-done.1, bf16[320,512]{1,0:T(8,128)(2,1)} %collective-permute-done.refs_2_, bf16[320,512]{1,0:T(8,128)(2,1)} %collective-permute-done.1.refs_3_, ...), custom_call_target="tpu_custom_call" | custom-call | tf_op jit(solution)/shard_map/sum/join/pallas_call | solution.py:268
  (1 shorter events, 0.0 us)
Async XLA Ops:
  0.6 28.8 %copy-start = (bf16[256,2048]{1,0:T(8,128)(2,1)S(1)}, bf16[256,2048]{1,0:T(8,128)(2,1)}, u32[]{:S(2)}) copy-start(bf16[256,2048]{1,0:T(8,128)(2,1)} %param.7) | copy-start | bytes 3145732
  5.2 125.4 %copy-start.2 = (bf16[2,128,128]{2,1,0:T(8,128)(2,1)S(1)}, bf16[2,128,128]{2,1,0:T(8,128)(2,1)}, u32[]{:S(2)}) copy-start(bf16[2,128,128]{2,1,0:T(8,128)(2,1)} %refs_2_.4) | copy-start | bytes 196612
  5.2 125.4 %all-to-all-start = ((bf16[512,16,128]{2,1,0:T(8,128)(2,1)}), bf16[512,16,128]{2,1,0:T(8,128)(2,1)S(1)}, u32[]{:S(2)}, u32[]{:S(2)}) async-start(bf16[512,16,128]{2,1,0:T(8,128)(2,1)} %mix.1), calls=%async_computation | async-start | bytes 4194304 | tf_op jit(solution)/shard_map/send/all_to_all | solution.py:215
  135.0 11.2 %copy-start.1 = (bf16[320,512]{1,0:T(8,128)(2,1)S(1)}, bf16[320,512]{1,0:T(8,128)(2,1)}, u32[]{:S(2)}) copy-start(bf16[320,512]{1,0:T(8,128)(2,1)} %get-tuple-element.9.refs_1_) | copy-start | bytes 983044
  135.1 112.1 %all-to-all-start.1 = ((bf16[512,16,128]{2,1,0:T(8,128)(2,1)}), bf16[512,16,128]{2,1,0:T(8,128)(2,1)S(1)}, u32[]{:S(2)}, u32[]{:S(2)}) async-start(bf16[512,16,128]{2,1,0:T(8,128)(2,1)} %bitcast.6), calls=%async_computation.1 | async-start | bytes 4194304 | tf_op jit(solution)/shard_map/return/all_to_all | solution.py:246
  146.2 129.3 %collective-permute-start.2 = (bf16[320,512]{1,0:T(8,128)(2,1)S(1)}, bf16[320,512]{1,0:T(8,128)(2,1)}, u32[]{:S(2)}, u32[]{:S(2)}) collective-permute-start(bf16[320,512]{1,0:T(8,128)(2,1)S(1)} %copy-done.1), channel_id=1, source_target_pairs={{0,384},{128,0},{256,128},{384,256},{1,385},{129,1},{257,129},{385... | collective-permute-start | bytes 983048 | tf_op jit(solution)/shard_map/gather_parts/ppermute | solution.py:244
  152.1 123.4 %collective-permute-start.1 = (bf16[320,512]{1,0:T(8,128)(2,1)S(1)}, bf16[320,512]{1,0:T(8,128)(2,1)}, u32[]{:S(2)}, u32[]{:S(2)}) collective-permute-start(bf16[320,512]{1,0:T(8,128)(2,1)S(1)} %copy-done.1), channel_id=1, source_target_pairs={{0,256},{128,384},{256,0},{384,128},{1,257},{129,385},{257,1},{385... | collective-permute-start | bytes 983048 | tf_op jit(solution)/shard_map/gather_parts/ppermute | solution.py:244
  154.1 121.5 %collective-permute-start = (bf16[320,512]{1,0:T(8,128)(2,1)S(1)}, bf16[320,512]{1,0:T(8,128)(2,1)}, u32[]{:S(2)}, u32[]{:S(2)}) collective-permute-start(bf16[320,512]{1,0:T(8,128)(2,1)S(1)} %copy-done.1), channel_id=1, source_target_pairs={{0,128},{128,256},{256,384},{384,0},{1,129},{129,257},{257,385},{3... | collective-permute-start | bytes 983048 | tf_op jit(solution)/shard_map/gather_parts/ppermute | solution.py:244

commit v4 on v3

--- a/solution.py
+++ b/solution.py
@@ -141,33 +141,33 @@
 
 def join_kernel(ranks, firsts_ref, *refs):
     pieces, refs = refs[:ranks], refs[ranks:]
-    kernel_out_ref, first_out_ref, second_out_ref, tails_ref, sems = refs
+    kernel_out_ref, first_out_ref, second_out_ref, held_ref, tails_ref, load_sems, store_sems = refs
     own, points, _ = second_out_ref.shape
     _, tail_rows, share = tails_ref.shape
     me = lax.axis_index("dp")
-    copies = []
+    loads, tails, stores = [], [], []
     for r in range(ranks):
         sender = lax.rem(me + ranks - r, ranks)
         chunk = pl.ds(pl.multiple_of(sender * share, share), share)
-        copies.append(
-            (
-                pltpu.make_async_copy(
-                    pieces[r].at[pl.ds(0, own * points), :], kernel_out_ref.at[:, chunk], sems.at[0, r]
-                ),
-                pltpu.make_async_copy(
-                    pieces[r].at[pl.ds(own * points, tail_rows), :], tails_ref.at[sender], sems.at[1, r]
-                ),
+        head = pl.ds(0, own * points)
+        loads.append(pltpu.make_async_copy(pieces[r].at[head, :], held_ref.at[r], load_sems.at[0, r]))
+        tails.append(
+            pltpu.make_async_copy(
+                pieces[r].at[pl.ds(own * points, tail_rows), :], tails_ref.at[sender], load_sems.at[1, r]
             )
         )
-    for pair in copies:
-        for copy in pair:
-            copy.start()
+        stores.append(pltpu.make_async_copy(held_ref.at[r], kernel_out_ref.at[:, chunk], store_sems.at[r]))
+    for copy in loads + tails:
+        copy.start()
+    for load, store in zip(loads, stores):
+        load.wait()
+        store.start()
     first = firsts_ref[0].astype(jnp.float32)
     for k in range(1, ranks):
         first += firsts_ref[k].astype(jnp.float32)
     first_out_ref[...] = first
-    for pair in copies:
-        pair[1].wait()
+    for copy in tails:
+        copy.wait()
     total = tails_ref[0].astype(jnp.float32)
     for k in range(1, ranks):
         total += tails_ref[k].astype(jnp.float32)
@@ -178,8 +178,8 @@
             second_out_ref[q, f * height : (f + 1) * height, :] = total[
                 q * height : (q + 1) * height, f * LANES : (f + 1) * LANES
             ]
-    for pair in copies:
-        pair[0].wait()
+    for copy in stores:
+        copy.wait()
 
 
 def in_hbm(array):
@@ -279,8 +279,10 @@
                 pl.BlockSpec(memory_space=pltpu.VMEM),
             ),
             scratch_shapes=[
+                pltpu.VMEM((ranks, own * points, share), jnp.bfloat16),
                 pltpu.VMEM((ranks, second_rows, share), jnp.bfloat16),
                 pltpu.SemaphoreType.DMA((2, ranks)),
+                pltpu.SemaphoreType.DMA((ranks,)),
             ],
             compiler_params=pltpu.CompilerParams(vmem_limit_bytes=32 * 1024 * 1024),
             name="join",

time: 303 us -> 280 us (0.924)
  Pallas kernels: 38.3 us -> 15.2 us
    pallas_call x1, Pallas kernels: 25.8 us -> 2.79 us  [shards(): pl.pallas_call(lambda *refs: join_kernel(ranks, *refs), out_shape=(jax.Sh...]
where the time goes in v4:
time: 280 us; the launch traced here: 278 us
  waiting for transfers between devices  192 us (69%)
  starting transfers between devices  45.5 us (16%)
  blocking collectives  25 us (9%)
  Pallas kernels  15.2 us (5%)
    all_to_all x1, waiting for transfers between devices, shards(): lax.all_to_all(mixed, ('dp', 'seq'), split_axis=0, concat_axis=0, tiled=T...  101 us
    all_to_all x1, waiting for transfers between devices, shards(): lax.all_to_all(back.reshape(ranks * members, rows, LANES), ('dp', 'seq'),...  90.8 us
    all_gather x1, blocking collectives, shards(): first_parts = lax.all_gather(first_part, 'dp')  25 us
    all_to_all x1, starting transfers between devices, shards(): lax.all_to_all(mixed, ('dp', 'seq'), split_axis=0, concat_axis=0, tiled=T...  24.3 us
    all_to_all x1, starting transfers between devices, shards(): lax.all_to_all(back.reshape(ranks * members, rows, LANES), ('dp', 'seq'),...  11.2 us
    ppermute x3, starting transfers between devices, shards(): lax.ppermute(part, 'dp', [(i, (i + r) % ranks) for i in range(ranks)])  10 us
  transfers between devices with their start and end apart: 5, of which 2 were waited for; matrix products, arithmetic and copies ran while one was open for 0% of the time, Pallas kernels for 1%

profile of v4, /device:TPU:1, one launch (start us, length us, event | category | flops | bytes accessed | tf_op | source)
XLA Modules:
  0.0 278.4 jit_solution(18366389952387784320)
XLA Ops:
  0.6 0.0 copy-start
  0.6 4.5 %mix.1 = bf16[512,16,128]{2,1,0:T(8,128)(2,1)} custom-call(bf16[1,256,256]{2,1,0:T(8,128)(2,1)} %refs_0_.1, bf16[1,256,2048]{2,1,0:T(8,128)(2,1)} %refs_1_.3, bf16[1,256,2048]{2,1,0:T(8,128)(2,1)} %refs_2_.5), custom_call_target="tpu_custom_call" | custom-call | tf_op jit(solution)/shard_map/mix/mix/pallas_call | solution.py:204
  5.2 0.0 copy-start.2
  5.2 24.3 %all-to-all-start = ((bf16[512,16,128]{2,1,0:T(8,128)(2,1)}), bf16[512,16,128]{2,1,0:T(8,128)(2,1)S(1)}, u32[]{:S(2)}, u32[]{:S(2)}) async-start(bf16[512,16,128]{2,1,0:T(8,128)(2,1)} %mix.1), calls=%async_computation | async-start | bytes 4194304 | tf_op jit(solution)/shard_map/send/all_to_all | solution.py:215
  29.5 0.0 copy-done
  29.5 101.1 %all-to-all-done = bf16[512,16,128]{2,1,0:T(8,128)(2,1)S(1)} async-done(((bf16[512,16,128]{2,1,0:T(8,128)(2,1)}), bf16[512,16,128]{2,1,0:T(8,128)(2,1)S(1)}, u32[]{:S(2)}, u32[]{:S(2)}) %all-to-all-start) | async-done | bytes 2097184 | tf_op jit(solution)/shard_map/send/all_to_all | solution.py:215
  130.6 0.0 copy-done.2
  130.6 4.5 %middle.1 = (bf16[4,128,16,128]{3,2,1,0:T(8,128)(2,1)}, bf16[320,512]{1,0:T(8,128)(2,1)}) custom-call(bf16[4,128,16,128]{3,2,1,0:T(8,128)(2,1)S(1)} %bitcast.4, bf16[256,512]{1,0:T(8,128)(2,1)S(1)} %constant_dynamic-slice_fusion.refs_1_, bf16[2,128,128]{2,1,0:T(8,128)(2,1)S(1)} %copy-done.2), custom_call_target="tpu_custom_call" | custom-call | tf_op jit(solution)/shard_map/middle/middle/pallas_call | solution.py:218
  135.0 0.0 copy-start.1
  135.1 11.2 %all-to-all-start.1 = ((bf16[512,16,128]{2,1,0:T(8,128)(2,1)}), bf16[512,16,128]{2,1,0:T(8,128)(2,1)S(1)}, u32[]{:S(2)}, u32[]{:S(2)}) async-start(bf16[512,16,128]{2,1,0:T(8,128)(2,1)} %bitcast.6), calls=%async_computation.1 | async-start | bytes 4194304 | tf_op jit(solution)/shard_map/return/all_to_all | solution.py:246
  146.2 0.0 copy-done.1
  146.2 5.9 %collective-permute-start.2 = (bf16[320,512]{1,0:T(8,128)(2,1)S(1)}, bf16[320,512]{1,0:T(8,128)(2,1)}, u32[]{:S(2)}, u32[]{:S(2)}) collective-permute-start(bf16[320,512]{1,0:T(8,128)(2,1)S(1)} %copy-done.1), channel_id=1, source_target_pairs={{0,384},{128,0},{256,128},{384,256},{1,385},{129,1},{257,129},{385... | collective-permute-start | bytes 983048 | tf_op jit(solution)/shard_map/gather_parts/ppermute | solution.py:244
  152.1 1.9 collective-permute-start.1
  154.1 2.2 collective-permute-start
  156.3 90.8 %all-to-all-done.1.refs_0_ = bf16[512,16,128]{2,1,0:T(8,128)(2,1)S(1)} async-done(((bf16[512,16,128]{2,1,0:T(8,128)(2,1)}), bf16[512,16,128]{2,1,0:T(8,128)(2,1)S(1)}, u32[]{:S(2)}, u32[]{:S(2)}) %all-to-all-start.1) | async-done | bytes 2097184 | tf_op jit(solution)/shard_map/return/all_to_all | solution.py:246
  247.1 3.5 %final.1 = bf16[256,256]{1,0:T(8,128)(2,1)S(1)} custom-call(bf16[512,16,128]{2,1,0:T(8,128)(2,1)S(1)} %all-to-all-done.1.refs_0_, bf16[1,256,2048]{2,1,0:T(8,128)(2,1)} %refs_1_.3, bf16[1,256,2048]{2,1,0:T(8,128)(2,1)} %refs_2_.5), custom_call_target="tpu_custom_call" | custom-call | tf_op jit(solution)/shard_map/final/final/pallas_call | solution.py:251
  250.6 25.0 %all-gather = bf16[1024,256]{1,0:T(8,128)(2,1)S(1)} all-gather(bf16[256,256]{1,0:T(8,128)(2,1)S(1)} %final.1), channel_id=2, replica_groups=mesh['dp'=4,'seq'=128] {'dp'}, dimensions={0}, use_global_device_ids=true | all-gather | bytes 655360 | tf_op jit(solution)/shard_map/sum/all_gather | solution.py:267
  275.6 0.0 collective-permute-done.2.refs_4_
  275.6 0.0 collective-permute-done.1.refs_3_
  275.6 0.0 collective-permute-done.refs_2_
  275.6 2.8 %join.1 = (bf16[256,2048]{1,0:T(8,128)(2,1)}, f32[256,256]{1,0:T(8,128)}, f32[2,128,128]{2,1,0:T(8,128)}) custom-call(bf16[4,256,256]{2,1,0:T(8,128)(2,1)S(1)} %bitcast.5, bf16[320,512]{1,0:T(8,128)(2,1)S(1)} %copy-done.1, bf16[320,512]{1,0:T(8,128)(2,1)} %collective-permute-done.refs_2_, bf16[320,512]{1,0:T(8,128)(2,1)} %collective-permute-done.1.refs_3_, ...), custom_call_target="tpu_custom_call" | custom-call | tf_op jit(solution)/shard_map/sum/join/pallas_call | solution.py:268
  (1 shorter events, 0.0 us)
Async XLA Ops:
  0.6 28.8 %copy-start = (bf16[256,2048]{1,0:T(8,128)(2,1)S(1)}, bf16[256,2048]{1,0:T(8,128)(2,1)}, u32[]{:S(2)}) copy-start(bf16[256,2048]{1,0:T(8,128)(2,1)} %param.7) | copy-start | bytes 3145732
  5.2 125.4 %copy-start.2 = (bf16[2,128,128]{2,1,0:T(8,128)(2,1)S(1)}, bf16[2,128,128]{2,1,0:T(8,128)(2,1)}, u32[]{:S(2)}) copy-start(bf16[2,128,128]{2,1,0:T(8,128)(2,1)} %refs_2_.4) | copy-start | bytes 196612
  5.2 125.4 %all-to-all-start = ((bf16[512,16,128]{2,1,0:T(8,128)(2,1)}), bf16[512,16,128]{2,1,0:T(8,128)(2,1)S(1)}, u32[]{:S(2)}, u32[]{:S(2)}) async-start(bf16[512,16,128]{2,1,0:T(8,128)(2,1)} %mix.1), calls=%async_computation | async-start | bytes 4194304 | tf_op jit(solution)/shard_map/send/all_to_all | solution.py:215
  135.0 11.2 %copy-start.1 = (bf16[320,512]{1,0:T(8,128)(2,1)S(1)}, bf16[320,512]{1,0:T(8,128)(2,1)}, u32[]{:S(2)}) copy-start(bf16[320,512]{1,0:T(8,128)(2,1)} %get-tuple-element.9.refs_1_) | copy-start | bytes 983044
  135.1 112.1 %all-to-all-start.1 = ((bf16[512,16,128]{2,1,0:T(8,128)(2,1)}), bf16[512,16,128]{2,1,0:T(8,128)(2,1)S(1)}, u32[]{:S(2)}, u32[]{:S(2)}) async-start(bf16[512,16,128]{2,1,0:T(8,128)(2,1)} %bitcast.6), calls=%async_computation.1 | async-start | bytes 4194304 | tf_op jit(solution)/shard_map/return/all_to_all | solution.py:246
  146.2 129.3 %collective-permute-start.2 = (bf16[320,512]{1,0:T(8,128)(2,1)S(1)}, bf16[320,512]{1,0:T(8,128)(2,1)}, u32[]{:S(2)}, u32[]{:S(2)}) collective-permute-start(bf16[320,512]{1,0:T(8,128)(2,1)S(1)} %copy-done.1), channel_id=1, source_target_pairs={{0,384},{128,0},{256,128},{384,256},{1,385},{129,1},{257,129},{385... | collective-permute-start | bytes 983048 | tf_op jit(solution)/shard_map/gather_parts/ppermute | solution.py:244
  152.1 123.4 %collective-permute-start.1 = (bf16[320,512]{1,0:T(8,128)(2,1)S(1)}, bf16[320,512]{1,0:T(8,128)(2,1)}, u32[]{:S(2)}, u32[]{:S(2)}) collective-permute-start(bf16[320,512]{1,0:T(8,128)(2,1)S(1)} %copy-done.1), channel_id=1, source_target_pairs={{0,256},{128,384},{256,0},{384,128},{1,257},{129,385},{257,1},{385... | collective-permute-start | bytes 983048 | tf_op jit(solution)/shard_map/gather_parts/ppermute | solution.py:244
  154.1 121.5 %collective-permute-start = (bf16[320,512]{1,0:T(8,128)(2,1)S(1)}, bf16[320,512]{1,0:T(8,128)(2,1)}, u32[]{:S(2)}, u32[]{:S(2)}) collective-permute-start(bf16[320,512]{1,0:T(8,128)(2,1)S(1)} %copy-done.1), channel_id=1, source_target_pairs={{0,128},{128,256},{256,384},{384,0},{1,129},{129,257},{257,385},{3... | collective-permute-start | bytes 983048 | tf_op jit(solution)/shard_map/gather_parts/ppermute | solution.py:244

commit v5 on v4

--- a/solution.py
+++ b/solution.py
@@ -52,19 +52,8 @@
     out_ref[...] = jnp.swapaxes(jnp.stack(pieces), 0, 1)
 
 
-def pack(blocks_ref, part_ref, start):
-    own, points, _ = blocks_ref.shape
-    fold = part_ref.shape[1] // LANES
-    height = points // fold
-    for q in range(own):
-        for f in range(fold):
-            part_ref[start + q * height : start + (q + 1) * height, f * LANES : (f + 1) * LANES] = blocks_ref[
-                q, f * height : (f + 1) * height, :
-            ].astype(jnp.bfloat16)
-
-
 def middle_kernel(
-    own, cols, shares, arrived_ref, kernel_ref, second_ref, back_ref, part_ref, total_ref, second_total_ref
+    own, cols, shares, arrived_ref, kernel_ref, second_ref, back_ref, part_ref, second_out_ref, total_ref, second_total_ref
 ):
     step = pl.program_id(0)
     last = pl.num_programs(0) - 1
@@ -96,14 +85,14 @@
 
     @pl.when(step == last)
     def _():
-        points = total_ref.shape[1]
+        points, members = second_total_ref.shape[1:]
         for q in range(own):
             part_ref[q * points : (q + 1) * points, :] = (total_ref[q] * seq_share).astype(jnp.bfloat16)
-        pack(second_total_ref, part_ref, own * points)
+            second_out_ref[:, q * members : (q + 1) * members] = second_total_ref[q].astype(jnp.bfloat16)
 
 
 def final_kernel(
-    own, cols, ranks, factor_share, returned_ref, tokens_ref, cotangent_ref, out_ref, total_ref, rows_ref, held_ref, sems
+    own, cols, ranks, factor_share, returned_ref, second_ref, tokens_ref, cotangent_ref, out_ref, total_ref, rows_ref, held_ref, sems
 ):
     groups = returned_ref.shape[0]
     share = cols * LANES
@@ -133,51 +122,37 @@
 
     @pl.when(step == last)
     def _():
+        height = rows_ref.shape[1]
+        out_ref[height:, :] = second_ref[...]
         for h in range(rows_ref.shape[0]):
             for q in range(own):
                 rows_ref[h, pl.ds(q, groups, stride=own), :] = total_ref[q, :, h * LANES : (h + 1) * LANES]
-            out_ref[:, h * LANES : (h + 1) * LANES] = (rows_ref[h] * factor_share).astype(jnp.bfloat16)
-
-
-def join_kernel(ranks, firsts_ref, *refs):
+            out_ref[:height, h * LANES : (h + 1) * LANES] = (rows_ref[h] * factor_share).astype(jnp.bfloat16)
+
+
+def join_kernel(ranks, gathered_ref, *refs):
     pieces, refs = refs[:ranks], refs[ranks:]
-    kernel_out_ref, first_out_ref, second_out_ref, held_ref, tails_ref, load_sems, store_sems = refs
-    own, points, _ = second_out_ref.shape
-    _, tail_rows, share = tails_ref.shape
+    kernel_out_ref, first_out_ref, second_out_ref, held_ref, load_sems, store_sems = refs
+    own, points, members = second_out_ref.shape
+    height = first_out_ref.shape[0]
+    share = held_ref.shape[2]
     me = lax.axis_index("dp")
-    loads, tails, stores = [], [], []
+    loads, stores = [], []
     for r in range(ranks):
-        sender = lax.rem(me + ranks - r, ranks)
-        chunk = pl.ds(pl.multiple_of(sender * share, share), share)
-        head = pl.ds(0, own * points)
-        loads.append(pltpu.make_async_copy(pieces[r].at[head, :], held_ref.at[r], load_sems.at[0, r]))
-        tails.append(
-            pltpu.make_async_copy(
-                pieces[r].at[pl.ds(own * points, tail_rows), :], tails_ref.at[sender], load_sems.at[1, r]
-            )
-        )
+        chunk = pl.ds(pl.multiple_of(lax.rem(me + ranks - r, ranks) * share, share), share)
+        loads.append(pltpu.make_async_copy(pieces[r], held_ref.at[r], load_sems.at[r]))
         stores.append(pltpu.make_async_copy(held_ref.at[r], kernel_out_ref.at[:, chunk], store_sems.at[r]))
-    for copy in loads + tails:
+    for copy in loads:
         copy.start()
     for load, store in zip(loads, stores):
         load.wait()
         store.start()
-    first = firsts_ref[0].astype(jnp.float32)
+    total = gathered_ref[0].astype(jnp.float32)
     for k in range(1, ranks):
-        first += firsts_ref[k].astype(jnp.float32)
-    first_out_ref[...] = first
-    for copy in tails:
-        copy.wait()
-    total = tails_ref[0].astype(jnp.float32)
-    for k in range(1, ranks):
-        total += tails_ref[k].astype(jnp.float32)
-    fold = share // LANES
-    height = points // fold
-    for q in range(own):
-        for f in range(fold):
-            second_out_ref[q, f * height : (f + 1) * height, :] = total[
-                q * height : (q + 1) * height, f * LANES : (f + 1) * LANES
-            ]
+        total += gathered_ref[k].astype(jnp.float32)
+    first_out_ref[...] = total[:height]
+    for q in range(own):
+        second_out_ref[q] = total[height:, q * members : (q + 1) * members]
     for copy in stores:
         copy.wait()
 
@@ -194,7 +169,6 @@
     cols = share // LANES
     rows = 2 * cols * own
     groups = local_rows // own
-    second_rows = own * points * members // share
     seq_share = 1.0 / math.sqrt(ranks)
     factor_share = 1.0 / math.sqrt(2.0 * channels * ranks)
     both = pl.BlockSpec((1, local_rows, share), lambda k: (0, 0, k))
@@ -215,11 +189,12 @@
         arrived = lax.all_to_all(mixed, ("dp", "seq"), split_axis=0, concat_axis=0, tiled=True)
     quarter = lax.dynamic_slice_in_dim(kernel, lax.axis_index("dp") * share, share, 1)
     with jax.named_scope("middle"):
-        back, part = pl.pallas_call(
+        back, part, second_part = pl.pallas_call(
             lambda *refs: middle_kernel(own, cols, (seq_share, factor_share), *refs),
             out_shape=(
                 pltpu.HBM((ranks, members, rows, LANES), jnp.bfloat16),
-                pltpu.HBM((own * points + second_rows, share), jnp.bfloat16),
+                pltpu.HBM((own * points, share), jnp.bfloat16),
+                pltpu.HBM((points, own * members), jnp.bfloat16),
             ),
             grid=(ranks,),
             in_specs=[
@@ -229,7 +204,8 @@
             ],
             out_specs=(
                 pl.BlockSpec((1, members, rows, LANES), lambda s: (s, 0, 0, 0)),
-                pl.BlockSpec((own * points + second_rows, share), lambda s: (0, 0)),
+                pl.BlockSpec((own * points, share), lambda s: (0, 0)),
+                pl.BlockSpec((points, own * members), lambda s: (0, 0)),
             ),
             scratch_shapes=[
                 pltpu.VMEM((own, points, share), jnp.float32),
@@ -248,12 +224,17 @@
         )
     with jax.named_scope("final"):
         whole = pl.BlockSpec(memory_space=pl.ANY)
-        first_part = pl.pallas_call(
+        factor_parts = pl.pallas_call(
             lambda *refs: final_kernel(own, cols, ranks, factor_share, *refs),
-            out_shape=jax.ShapeDtypeStruct((local_rows, local_rows), jnp.bfloat16),
+            out_shape=jax.ShapeDtypeStruct((local_rows + points, local_rows), jnp.bfloat16),
             grid=(ranks,),
-            in_specs=[pl.BlockSpec((members, rows, LANES), lambda k: (k, 0, 0)), whole, whole],
-            out_specs=pl.BlockSpec((local_rows, local_rows), lambda k: (0, 0)),
+            in_specs=[
+                pl.BlockSpec((members, rows, LANES), lambda k: (k, 0, 0)),
+                pl.BlockSpec((points, own * members), lambda k: (0, 0)),
+                whole,
+                whole,
+            ],
+            out_specs=pl.BlockSpec((local_rows + points, local_rows), lambda k: (0, 0)),
             scratch_shapes=[
                 pltpu.VMEM((own, groups, local_rows), jnp.float32),
                 pltpu.VMEM((local_rows // LANES, local_rows, LANES), jnp.float32),
@@ -262,9 +243,9 @@
             ],
             compiler_params=params,
             name="final",
-        )(returned, in_hbm(tokens), in_hbm(cotangent))
+        )(returned, second_part, in_hbm(tokens), in_hbm(cotangent))
     with jax.named_scope("sum"):
-        first_parts = lax.all_gather(first_part, "dp")
+        gathered = lax.all_gather(factor_parts, "dp")
         kernel_out, first_out, second_out = pl.pallas_call(
             lambda *refs: join_kernel(ranks, *refs),
             out_shape=(
@@ -280,13 +261,12 @@
             ),
             scratch_shapes=[
                 pltpu.VMEM((ranks, own * points, share), jnp.bfloat16),
-                pltpu.VMEM((ranks, second_rows, share), jnp.bfloat16),
-                pltpu.SemaphoreType.DMA((2, ranks)),
+                pltpu.SemaphoreType.DMA((ranks,)),
                 pltpu.SemaphoreType.DMA((ranks,)),
             ],
             compiler_params=pltpu.CompilerParams(vmem_limit_bytes=32 * 1024 * 1024),
             name="join",
-        )(first_parts, *pieces)
+        )(gathered, *pieces)
     return kernel_out, first_out[None], second_out
 
 

time: 280 us -> 277 us (0.989)
  blocking collectives: 25 us -> 21.2 us
    all_gather x1, blocking collectives: 25 us -> 21.2 us  [shards(): gathered = lax.all_gather(factor_parts, 'dp')]
where the time goes in v5:
time: 277 us; the launch traced here: 275 us
  waiting for transfers between devices  192 us (69%)
  starting transfers between devices  45.5 us (16%)
  blocking collectives  21.2 us (8%)
  Pallas kernels  15.2 us (5%)
    all_to_all x1, waiting for transfers between devices, shards(): lax.all_to_all(mixed, ('dp', 'seq'), split_axis=0, concat_axis=0, tiled=T...  101 us
    all_to_all x1, waiting for transfers between devices, shards(): lax.all_to_all(back.reshape(ranks * members, rows, LANES), ('dp', 'seq'),...  90.8 us
    all_to_all x1, starting transfers between devices, shards(): lax.all_to_all(mixed, ('dp', 'seq'), split_axis=0, concat_axis=0, tiled=T...  24.3 us
    all_gather x1, blocking collectives, shards(): gathered = lax.all_gather(factor_parts, 'dp')  21.2 us
    all_to_all x1, starting transfers between devices, shards(): lax.all_to_all(back.reshape(ranks * members, rows, LANES), ('dp', 'seq'),...  11.2 us
    ppermute x3, starting transfers between devices, shards(): lax.ppermute(part, 'dp', [(i, (i + r) % ranks) for i in range(ranks)])  10 us
  transfers between devices with their start and end apart: 5, of which 2 were waited for; matrix products, arithmetic and copies ran while one was open for 0% of the time, Pallas kernels for 1%

profile of v5, /device:TPU:1, one launch (start us, length us, event | category | flops | bytes accessed | tf_op | source)
XLA Modules:
  0.0 274.6 jit_solution(10683648832644494066)
XLA Ops:
  0.6 0.0 copy-start
  0.6 4.5 %mix.1 = bf16[512,16,128]{2,1,0:T(8,128)(2,1)} custom-call(bf16[1,256,256]{2,1,0:T(8,128)(2,1)} %refs_0_.1, bf16[1,256,2048]{2,1,0:T(8,128)(2,1)} %refs_2_.5, bf16[1,256,2048]{2,1,0:T(8,128)(2,1)} %refs_3_.1), custom_call_target="tpu_custom_call" | custom-call | tf_op jit(solution)/shard_map/mix/mix/pallas_call | solution.py:178
  5.2 0.0 copy-start.3
  5.2 24.3 %all-to-all-start = ((bf16[512,16,128]{2,1,0:T(8,128)(2,1)}), bf16[512,16,128]{2,1,0:T(8,128)(2,1)S(1)}, u32[]{:S(2)}, u32[]{:S(2)}) async-start(bf16[512,16,128]{2,1,0:T(8,128)(2,1)} %mix.1), calls=%async_computation | async-start | bytes 4194304 | tf_op jit(solution)/shard_map/send/all_to_all | solution.py:189
  29.5 0.0 copy-done
  29.5 101.1 %all-to-all-done = bf16[512,16,128]{2,1,0:T(8,128)(2,1)S(1)} async-done(((bf16[512,16,128]{2,1,0:T(8,128)(2,1)}), bf16[512,16,128]{2,1,0:T(8,128)(2,1)S(1)}, u32[]{:S(2)}, u32[]{:S(2)}) %all-to-all-start) | async-done | bytes 2097184 | tf_op jit(solution)/shard_map/send/all_to_all | solution.py:189
  130.6 0.0 copy-done.3
  130.6 4.5 %middle.1 = (bf16[4,128,16,128]{3,2,1,0:T(8,128)(2,1)}, bf16[256,512]{1,0:T(8,128)(2,1)}, bf16[128,256]{1,0:T(8,128)(2,1)}) custom-call(bf16[4,128,16,128]{3,2,1,0:T(8,128)(2,1)S(1)} %bitcast.4, bf16[256,512]{1,0:T(8,128)(2,1)S(1)} %constant_dynamic-slice_fusion.refs_1_, bf16[2,128,128]{2,1,0:T(8,128)(2,1)S(1)} %copy-done.3), custom_call_target="tpu_custom_call" | custom-call | tf_op jit(solution)/shard_map/middle/middle/pallas_call | solution.py:192
  135.1 0.0 copy-start.1
  135.1 0.0 copy-start.2
  135.1 11.2 %all-to-all-start.1 = ((bf16[512,16,128]{2,1,0:T(8,128)(2,1)}), bf16[512,16,128]{2,1,0:T(8,128)(2,1)S(1)}, u32[]{:S(2)}, u32[]{:S(2)}) async-start(bf16[512,16,128]{2,1,0:T(8,128)(2,1)} %bitcast.6), calls=%async_computation.1 | async-start | bytes 4194304 | tf_op jit(solution)/shard_map/return/all_to_all | solution.py:222
  146.3 0.0 copy-done.1
  146.3 5.9 %collective-permute-start.2 = (bf16[256,512]{1,0:T(8,128)(2,1)S(1)}, bf16[256,512]{1,0:T(8,128)(2,1)}, u32[]{:S(2)}, u32[]{:S(2)}) collective-permute-start(bf16[256,512]{1,0:T(8,128)(2,1)S(1)} %copy-done.1), channel_id=1, source_target_pairs={{0,384},{128,0},{256,128},{384,256},{1,385},{129,1},{257,129},{385... | collective-permute-start | bytes 786440 | tf_op jit(solution)/shard_map/gather_parts/ppermute | solution.py:220
  152.2 1.9 collective-permute-start.1
  154.1 2.2 collective-permute-start
  156.3 90.8 %all-to-all-done.1.refs_0_ = bf16[512,16,128]{2,1,0:T(8,128)(2,1)S(1)} async-done(((bf16[512,16,128]{2,1,0:T(8,128)(2,1)}), bf16[512,16,128]{2,1,0:T(8,128)(2,1)S(1)}, u32[]{:S(2)}, u32[]{:S(2)}) %all-to-all-start.1) | async-done | bytes 2097184 | tf_op jit(solution)/shard_map/return/all_to_all | solution.py:222
  247.2 0.0 copy-done.2
  247.2 3.5 %final.1 = bf16[384,256]{1,0:T(8,128)(2,1)S(1)} custom-call(bf16[512,16,128]{2,1,0:T(8,128)(2,1)S(1)} %all-to-all-done.1.refs_0_, bf16[128,256]{1,0:T(8,128)(2,1)S(1)} %copy-done.2, bf16[1,256,2048]{2,1,0:T(8,128)(2,1)} %refs_2_.5, bf16[1,256,2048]{2,1,0:T(8,128)(2,1)} %refs_3_.1), custom_call_target="tpu_custom_call" | custom-call | tf_op jit(solution)/shard_map/final/final/pallas_call | solution.py:227
  250.6 21.2 %all-gather = bf16[1536,256]{1,0:T(8,128)(2,1)S(1)} all-gather(bf16[384,256]{1,0:T(8,128)(2,1)S(1)} %final.1), channel_id=2, replica_groups=mesh['dp'=4,'seq'=128] {'dp'}, dimensions={0}, use_global_device_ids=true | all-gather | bytes 983040 | tf_op jit(solution)/shard_map/sum/all_gather | solution.py:248
  271.9 0.0 collective-permute-done.2.refs_4_
  271.9 0.0 collective-permute-done.1.refs_3_
  271.9 0.0 collective-permute-done.refs_2_
  271.9 2.8 %join.1 = (bf16[256,2048]{1,0:T(8,128)(2,1)}, f32[256,256]{1,0:T(8,128)}, f32[2,128,128]{2,1,0:T(8,128)}) custom-call(bf16[4,384,256]{2,1,0:T(8,128)(2,1)S(1)} %bitcast.5, bf16[256,512]{1,0:T(8,128)(2,1)S(1)} %copy-done.1, bf16[256,512]{1,0:T(8,128)(2,1)} %collective-permute-done.refs_2_, bf16[256,512]{1,0:T(8,128)(2,1)} %collective-permute-done.1.refs_3_, ...), custom_call_target="tpu_custom_call" | custom-call | tf_op jit(solution)/shard_map/sum/join/pallas_call | solution.py:249
  (1 shorter events, 0.0 us)
Async XLA Ops:
  0.6 28.9 %copy-start = (bf16[256,2048]{1,0:T(8,128)(2,1)S(1)}, bf16[256,2048]{1,0:T(8,128)(2,1)}, u32[]{:S(2)}) copy-start(bf16[256,2048]{1,0:T(8,128)(2,1)} %param.7) | copy-start | bytes 3145732
  5.2 125.4 %copy-start.3 = (bf16[2,128,128]{2,1,0:T(8,128)(2,1)S(1)}, bf16[2,128,128]{2,1,0:T(8,128)(2,1)}, u32[]{:S(2)}) copy-start(bf16[2,128,128]{2,1,0:T(8,128)(2,1)} %refs_2_.4) | copy-start | bytes 196612
  5.2 125.4 %all-to-all-start = ((bf16[512,16,128]{2,1,0:T(8,128)(2,1)}), bf16[512,16,128]{2,1,0:T(8,128)(2,1)S(1)}, u32[]{:S(2)}, u32[]{:S(2)}) async-start(bf16[512,16,128]{2,1,0:T(8,128)(2,1)} %mix.1), calls=%async_computation | async-start | bytes 4194304 | tf_op jit(solution)/shard_map/send/all_to_all | solution.py:189
  135.1 11.2 %copy-start.1 = (bf16[256,512]{1,0:T(8,128)(2,1)S(1)}, bf16[256,512]{1,0:T(8,128)(2,1)}, u32[]{:S(2)}) copy-start(bf16[256,512]{1,0:T(8,128)(2,1)} %get-tuple-element.11.refs_1_) | copy-start | bytes 786436
  135.1 112.1 %copy-start.2 = (bf16[128,256]{1,0:T(8,128)(2,1)S(1)}, bf16[128,256]{1,0:T(8,128)(2,1)}, u32[]{:S(2)}) copy-start(bf16[128,256]{1,0:T(8,128)(2,1)} %get-tuple-element.10.refs_1_) | copy-start | bytes 196612
  135.1 112.1 %all-to-all-start.1 = ((bf16[512,16,128]{2,1,0:T(8,128)(2,1)}), bf16[512,16,128]{2,1,0:T(8,128)(2,1)S(1)}, u32[]{:S(2)}, u32[]{:S(2)}) async-start(bf16[512,16,128]{2,1,0:T(8,128)(2,1)} %bitcast.6), calls=%async_computation.1 | async-start | bytes 4194304 | tf_op jit(solution)/shard_map/return/all_to_all | solution.py:222
  146.3 125.6 %collective-permute-start.2 = (bf16[256,512]{1,0:T(8,128)(2,1)S(1)}, bf16[256,512]{1,0:T(8,128)(2,1)}, u32[]{:S(2)}, u32[]{:S(2)}) collective-permute-start(bf16[256,512]{1,0:T(8,128)(2,1)S(1)} %copy-done.1), channel_id=1, source_target_pairs={{0,384},{128,0},{256,128},{384,256},{1,385},{129,1},{257,129},{385... | collective-permute-start | bytes 786440 | tf_op jit(solution)/shard_map/gather_parts/ppermute | solution.py:220
  152.2 119.7 %collective-permute-start.1 = (bf16[256,512]{1,0:T(8,128)(2,1)S(1)}, bf16[256,512]{1,0:T(8,128)(2,1)}, u32[]{:S(2)}, u32[]{:S(2)}) collective-permute-start(bf16[256,512]{1,0:T(8,128)(2,1)S(1)} %copy-done.1), channel_id=1, source_target_pairs={{0,256},{128,384},{256,0},{384,128},{1,257},{129,385},{257,1},{385... | collective-permute-start | bytes 786440 | tf_op jit(solution)/shard_map/gather_parts/ppermute | solution.py:220
  154.1 117.8 %collective-permute-start = (bf16[256,512]{1,0:T(8,128)(2,1)S(1)}, bf16[256,512]{1,0:T(8,128)(2,1)}, u32[]{:S(2)}, u32[]{:S(2)}) collective-permute-start(bf16[256,512]{1,0:T(8,128)(2,1)S(1)} %copy-done.1), channel_id=1, source_target_pairs={{0,128},{128,256},{256,384},{384,0},{1,129},{129,257},{257,385},{3... | collective-permute-start | bytes 786440 | tf_op jit(solution)/shard_map/gather_parts/ppermute | solution.py:220

commit v6 on v5

--- a/solution.py
+++ b/solution.py
@@ -28,14 +28,28 @@
     ]
 
 
-def mix_kernel(own, cols, first_ref, tokens_ref, cotangent_ref, out_ref, factor_ref):
+def loads(refs, held_ref, sems, share, k):
+    chunk = pl.ds(pl.multiple_of(k * share, share), share)
+    return [
+        pltpu.make_async_copy(ref.at[0, :, chunk], held_ref.at[t, k], sems.at[t, k]) for t, ref in enumerate(refs)
+    ]
+
+
+def mix_kernel(own, cols, ranks, first_ref, tokens_ref, cotangent_ref, out_ref, factor_ref, held_ref, sems):
     groups = out_ref.shape[0]
-
-    @pl.when(pl.program_id(0) == 0)
-    def _():
+    step = pl.program_id(0)
+    sources = (tokens_ref, cotangent_ref)
+
+    @pl.when(step == 0)
+    def _():
+        for k in range(ranks):
+            for copy in loads(sources, held_ref, sems, cols * LANES, k):
+                copy.start()
         for h in range(factor_ref.shape[0]):
             factor_ref[h] = first_ref[0, :, h * LANES : (h + 1) * LANES].astype(jnp.float32)
 
+    for copy in loads(sources, held_ref, sems, cols * LANES, step):
+        copy.wait()
     pieces = [None] * out_ref.shape[1]
     for q in range(own):
         factor = jnp.concatenate(
@@ -45,8 +59,8 @@
             ],
             axis=1,
         )
-        for t, ref in enumerate((tokens_ref, cotangent_ref)):
-            mixed = nn(factor, ref[0]).astype(jnp.bfloat16)
+        for t in range(2):
+            mixed = nn(factor, held_ref[t, step]).astype(jnp.bfloat16)
             for ci in range(cols):
                 pieces[(t * cols + ci) * own + q] = mixed[:, ci * LANES : (ci + 1) * LANES]
     out_ref[...] = jnp.swapaxes(jnp.stack(pieces), 0, 1)
@@ -64,7 +78,7 @@
         total_ref[...] = jnp.zeros_like(total_ref)
         second_total_ref[...] = jnp.zeros_like(second_total_ref)
 
-    arrived = jnp.swapaxes(arrived_ref[0], 0, 1)
+    arrived = jnp.swapaxes(arrived_ref[step], 0, 1)
     pieces = [None] * arrived.shape[0]
     for q in range(own):
         factor = second_ref[q]
@@ -94,27 +108,22 @@
 def final_kernel(
     own, cols, ranks, factor_share, returned_ref, second_ref, tokens_ref, cotangent_ref, out_ref, total_ref, rows_ref, held_ref, sems
 ):
-    groups = returned_ref.shape[0]
+    groups = returned_ref.shape[1]
     share = cols * LANES
     step = pl.program_id(0)
     last = pl.num_programs(0) - 1
 
-    def loads(k):
-        chunk = pl.ds(pl.multiple_of(k * share, share), share)
-        return [
-            pltpu.make_async_copy(ref.at[0, :, chunk], held_ref.at[t, k], sems.at[t, k])
-            for t, ref in enumerate((tokens_ref, cotangent_ref))
-        ]
+    sources = (tokens_ref, cotangent_ref)
 
     @pl.when(step == 0)
     def _():
         for k in range(ranks):
-            for copy in loads(k):
+            for copy in loads(sources, held_ref, sems, share, k):
                 copy.start()
         total_ref[...] = jnp.zeros_like(total_ref)
 
-    returned = jnp.swapaxes(returned_ref[...], 0, 1)
-    for copy in loads(step):
+    returned = jnp.swapaxes(returned_ref[step], 0, 1)
+    for copy in loads(sources, held_ref, sems, share, step):
         copy.wait()
     for q in range(own):
         spread, pulled_back = beside(returned, own, cols, q)
@@ -171,17 +180,22 @@
     groups = local_rows // own
     seq_share = 1.0 / math.sqrt(ranks)
     factor_share = 1.0 / math.sqrt(2.0 * channels * ranks)
-    both = pl.BlockSpec((1, local_rows, share), lambda k: (0, 0, k))
+    whole = pl.BlockSpec(memory_space=pl.ANY)
+    vmem = pl.BlockSpec(memory_space=pltpu.VMEM)
     params = pltpu.CompilerParams(dimension_semantics=("arbitrary",), vmem_limit_bytes=32 * 1024 * 1024)
 
     with jax.named_scope("mix"):
         mixed = pl.pallas_call(
-            lambda *refs: mix_kernel(own, cols, *refs),
+            lambda *refs: mix_kernel(own, cols, ranks, *refs),
             out_shape=pltpu.HBM((ranks * members, rows, LANES), jnp.bfloat16),
             grid=(ranks,),
-            in_specs=[pl.BlockSpec((1, local_rows, local_rows), lambda k: (0, 0, 0)), both, both],
+            in_specs=[pl.BlockSpec((1, local_rows, local_rows), lambda k: (0, 0, 0)), whole, whole],
             out_specs=pl.BlockSpec((members, rows, LANES), lambda k: (k, 0, 0)),
-            scratch_shapes=[pltpu.VMEM((local_rows // LANES, local_rows, LANES), jnp.float32)],
+            scratch_shapes=[
+                pltpu.VMEM((local_rows // LANES, local_rows, LANES), jnp.float32),
+                pltpu.VMEM((2, ranks, local_rows, share), jnp.bfloat16),
+                pltpu.SemaphoreType.DMA((2, ranks)),
+            ],
             compiler_params=params,
             name="mix",
         )(in_hbm(first_factor), in_hbm(tokens), in_hbm(cotangent))
@@ -197,11 +211,7 @@
                 pltpu.HBM((points, own * members), jnp.bfloat16),
             ),
             grid=(ranks,),
-            in_specs=[
-                pl.BlockSpec((1, members, rows, LANES), lambda s: (s, 0, 0, 0)),
-                pl.BlockSpec((own * points, share), lambda s: (0, 0)),
-                pl.BlockSpec((own, points, members), lambda s: (0, 0, 0)),
-            ],
+            in_specs=[vmem, vmem, vmem],
             out_specs=(
                 pl.BlockSpec((1, members, rows, LANES), lambda s: (s, 0, 0, 0)),
                 pl.BlockSpec((own * points, share), lambda s: (0, 0)),
@@ -223,17 +233,11 @@
             back.reshape(ranks * members, rows, LANES), ("dp", "seq"), split_axis=0, concat_axis=0, tiled=True
         )
     with jax.named_scope("final"):
-        whole = pl.BlockSpec(memory_space=pl.ANY)
         factor_parts = pl.pallas_call(
             lambda *refs: final_kernel(own, cols, ranks, factor_share, *refs),
             out_shape=jax.ShapeDtypeStruct((local_rows + points, local_rows), jnp.bfloat16),
             grid=(ranks,),
-            in_specs=[
-                pl.BlockSpec((members, rows, LANES), lambda k: (k, 0, 0)),
-                pl.BlockSpec((points, own * members), lambda k: (0, 0)),
-                whole,
-                whole,
-            ],
+            in_specs=[vmem, vmem, whole, whole],
             out_specs=pl.BlockSpec((local_rows + points, local_rows), lambda k: (0, 0)),
             scratch_shapes=[
                 pltpu.VMEM((own, groups, local_rows), jnp.float32),
@@ -243,7 +247,7 @@
             ],
             compiler_params=params,
             name="final",
-        )(returned, second_part, in_hbm(tokens), in_hbm(cotangent))
+        )(returned.reshape(ranks, members, rows, LANES), second_part, in_hbm(tokens), in_hbm(cotangent))
     with jax.named_scope("sum"):
         gathered = lax.all_gather(factor_parts, "dp")
         kernel_out, first_out, second_out = pl.pallas_call(
@@ -253,7 +257,7 @@
                 jax.ShapeDtypeStruct((local_rows, local_rows), jnp.float32),
                 jax.ShapeDtypeStruct((own, points, members), jnp.float32),
             ),
-            in_specs=[pl.BlockSpec(memory_space=pltpu.VMEM)] + [whole] * ranks,
+            in_specs=[vmem] + [whole] * ranks,
             out_specs=(
                 whole,
                 pl.BlockSpec(memory_space=pltpu.VMEM),

time: 277 us -> 277 us (level)
  no operation moved by 1% of the time
where the time goes in v6:
time: 277 us; the launch traced here: 275 us
  waiting for transfers between devices  192 us (69%)
  starting transfers between devices  45.5 us (16%)
  blocking collectives  20.7 us (7%)
  Pallas kernels  15.8 us (6%)
    all_to_all x1, waiting for transfers between devices, shards(): lax.all_to_all(mixed, ('dp', 'seq'), split_axis=0, concat_axis=0, tiled=T...  101 us
    all_to_all x1, waiting for transfers between devices, shards(): lax.all_to_all(back.reshape(ranks * members, rows, LANES), ('dp', 'seq'),...  90.8 us
    all_to_all x1, starting transfers between devices, shards(): lax.all_to_all(mixed, ('dp', 'seq'), split_axis=0, concat_axis=0, tiled=T...  24.3 us
    all_gather x1, blocking collectives, shards(): gathered = lax.all_gather(factor_parts, 'dp')  20.7 us
    all_to_all x1, starting transfers between devices, shards(): lax.all_to_all(back.reshape(ranks * members, rows, LANES), ('dp', 'seq'),...  11.2 us
    ppermute x3, starting transfers between devices, shards(): lax.ppermute(part, 'dp', [(i, (i + r) % ranks) for i in range(ranks)])  10 us
  transfers between devices with their start and end apart: 5, of which 2 were waited for; matrix products, arithmetic and copies ran while one was open for 0% of the time, Pallas kernels for 1%

profile of v6, /device:TPU:1, one launch (start us, length us, event | category | flops | bytes accessed | tf_op | source)
XLA Modules:
  0.0 274.7 jit_solution(13527273434948791635)
XLA Ops:
  0.6 0.0 copy-start
  0.6 4.7 %mix.1 = bf16[512,16,128]{2,1,0:T(8,128)(2,1)} custom-call(bf16[1,256,256]{2,1,0:T(8,128)(2,1)} %refs_0_.1, bf16[1,256,2048]{2,1,0:T(8,128)(2,1)} %refs_2_.5, bf16[1,256,2048]{2,1,0:T(8,128)(2,1)} %refs_3_.1), custom_call_target="tpu_custom_call" | custom-call | tf_op jit(solution)/shard_map/mix/mix/pallas_call | solution.py:188
  5.4 0.0 copy-start.3
  5.4 24.3 %all-to-all-start = ((bf16[512,16,128]{2,1,0:T(8,128)(2,1)}), bf16[512,16,128]{2,1,0:T(8,128)(2,1)S(1)}, u32[]{:S(2)}, u32[]{:S(2)}) async-start(bf16[512,16,128]{2,1,0:T(8,128)(2,1)} %mix.1), calls=%async_computation | async-start | bytes 4194304 | tf_op jit(solution)/shard_map/send/all_to_all | solution.py:203
  29.7 0.0 copy-done
  29.8 101.1 %all-to-all-done = bf16[512,16,128]{2,1,0:T(8,128)(2,1)S(1)} async-done(((bf16[512,16,128]{2,1,0:T(8,128)(2,1)}), bf16[512,16,128]{2,1,0:T(8,128)(2,1)S(1)}, u32[]{:S(2)}, u32[]{:S(2)}) %all-to-all-start) | async-done | bytes 2097184 | tf_op jit(solution)/shard_map/send/all_to_all | solution.py:203
  130.8 0.0 copy-done.3
  130.8 4.5 %middle.1 = (bf16[4,128,16,128]{3,2,1,0:T(8,128)(2,1)}, bf16[256,512]{1,0:T(8,128)(2,1)}, bf16[128,256]{1,0:T(8,128)(2,1)}) custom-call(bf16[4,128,16,128]{3,2,1,0:T(8,128)(2,1)S(1)} %bitcast.5, bf16[256,512]{1,0:T(8,128)(2,1)S(1)} %constant_dynamic-slice_fusion.refs_1_, bf16[2,128,128]{2,1,0:T(8,128)(2,1)S(1)} %copy-done.3), custom_call_target="tpu_custom_call" | custom-call | tf_op jit(solution)/shard_map/middle/middle/pallas_call | solution.py:206
  135.3 0.0 copy-start.1
  135.3 0.0 copy-start.2
  135.3 11.2 %all-to-all-start.1 = ((bf16[512,16,128]{2,1,0:T(8,128)(2,1)}), bf16[512,16,128]{2,1,0:T(8,128)(2,1)S(1)}, u32[]{:S(2)}, u32[]{:S(2)}) async-start(bf16[512,16,128]{2,1,0:T(8,128)(2,1)} %bitcast.8), calls=%async_computation.1 | async-start | bytes 4194304 | tf_op jit(solution)/shard_map/return/all_to_all | solution.py:232
  146.5 0.0 copy-done.1
  146.5 5.9 %collective-permute-start.2 = (bf16[256,512]{1,0:T(8,128)(2,1)S(1)}, bf16[256,512]{1,0:T(8,128)(2,1)}, u32[]{:S(2)}, u32[]{:S(2)}) collective-permute-start(bf16[256,512]{1,0:T(8,128)(2,1)S(1)} %copy-done.1), channel_id=1, source_target_pairs={{0,384},{128,0},{256,128},{384,256},{1,385},{129,1},{257,129},{385... | collective-permute-start | bytes 786440 | tf_op jit(solution)/shard_map/gather_parts/ppermute | solution.py:230
  152.4 1.9 collective-permute-start.1
  154.3 2.2 collective-permute-start
  156.5 90.8 %all-to-all-done.1 = bf16[512,16,128]{2,1,0:T(8,128)(2,1)S(1)} async-done(((bf16[512,16,128]{2,1,0:T(8,128)(2,1)}), bf16[512,16,128]{2,1,0:T(8,128)(2,1)S(1)}, u32[]{:S(2)}, u32[]{:S(2)}) %all-to-all-start.1) | async-done | bytes 2097184 | tf_op jit(solution)/shard_map/return/all_to_all | solution.py:232
  247.4 0.0 copy-done.2
  247.4 3.8 %final.1 = bf16[384,256]{1,0:T(8,128)(2,1)S(1)} custom-call(bf16[4,128,16,128]{3,2,1,0:T(8,128)(2,1)S(1)} %bitcast.6, bf16[128,256]{1,0:T(8,128)(2,1)S(1)} %copy-done.2, bf16[1,256,2048]{2,1,0:T(8,128)(2,1)} %refs_2_.5, bf16[1,256,2048]{2,1,0:T(8,128)(2,1)} %refs_3_.1), custom_call_target="tpu_custom_call" | custom-call | tf_op jit(solution)/shard_map/final/final/pallas_call | solution.py:236
  251.2 20.7 %all-gather = bf16[1536,256]{1,0:T(8,128)(2,1)S(1)} all-gather(bf16[384,256]{1,0:T(8,128)(2,1)S(1)} %final.1), channel_id=2, replica_groups=mesh['dp'=4,'seq'=128] {'dp'}, dimensions={0}, use_global_device_ids=true | all-gather | bytes 983040 | tf_op jit(solution)/shard_map/sum/all_gather | solution.py:252
  272.0 0.0 collective-permute-done.2.refs_4_
  272.0 0.0 collective-permute-done.1.refs_3_
  272.0 0.0 collective-permute-done.refs_2_
  272.0 2.8 %join.1 = (bf16[256,2048]{1,0:T(8,128)(2,1)}, f32[256,256]{1,0:T(8,128)}, f32[2,128,128]{2,1,0:T(8,128)}) custom-call(bf16[4,384,256]{2,1,0:T(8,128)(2,1)S(1)} %bitcast.7, bf16[256,512]{1,0:T(8,128)(2,1)S(1)} %copy-done.1, bf16[256,512]{1,0:T(8,128)(2,1)} %collective-permute-done.refs_2_, bf16[256,512]{1,0:T(8,128)(2,1)} %collective-permute-done.1.refs_3_, ...), custom_call_target="tpu_custom_call" | custom-call | tf_op jit(solution)/shard_map/sum/join/pallas_call | solution.py:253
  (1 shorter events, 0.0 us)
Async XLA Ops:
  0.6 29.1 %copy-start = (bf16[256,2048]{1,0:T(8,128)(2,1)S(1)}, bf16[256,2048]{1,0:T(8,128)(2,1)}, u32[]{:S(2)}) copy-start(bf16[256,2048]{1,0:T(8,128)(2,1)} %param.7) | copy-start | bytes 3145732
  5.4 125.4 %copy-start.3 = (bf16[2,128,128]{2,1,0:T(8,128)(2,1)S(1)}, bf16[2,128,128]{2,1,0:T(8,128)(2,1)}, u32[]{:S(2)}) copy-start(bf16[2,128,128]{2,1,0:T(8,128)(2,1)} %refs_2_.4) | copy-start | bytes 196612
  5.4 125.4 %all-to-all-start = ((bf16[512,16,128]{2,1,0:T(8,128)(2,1)}), bf16[512,16,128]{2,1,0:T(8,128)(2,1)S(1)}, u32[]{:S(2)}, u32[]{:S(2)}) async-start(bf16[512,16,128]{2,1,0:T(8,128)(2,1)} %mix.1), calls=%async_computation | async-start | bytes 4194304 | tf_op jit(solution)/shard_map/send/all_to_all | solution.py:203
  135.3 11.2 %copy-start.1 = (bf16[256,512]{1,0:T(8,128)(2,1)S(1)}, bf16[256,512]{1,0:T(8,128)(2,1)}, u32[]{:S(2)}) copy-start(bf16[256,512]{1,0:T(8,128)(2,1)} %get-tuple-element.11.refs_1_) | copy-start | bytes 786436
  135.3 112.1 %copy-start.2 = (bf16[128,256]{1,0:T(8,128)(2,1)S(1)}, bf16[128,256]{1,0:T(8,128)(2,1)}, u32[]{:S(2)}) copy-start(bf16[128,256]{1,0:T(8,128)(2,1)} %get-tuple-element.10.refs_1_) | copy-start | bytes 196612
  135.3 112.1 %all-to-all-start.1 = ((bf16[512,16,128]{2,1,0:T(8,128)(2,1)}), bf16[512,16,128]{2,1,0:T(8,128)(2,1)S(1)}, u32[]{:S(2)}, u32[]{:S(2)}) async-start(bf16[512,16,128]{2,1,0:T(8,128)(2,1)} %bitcast.8), calls=%async_computation.1 | async-start | bytes 4194304 | tf_op jit(solution)/shard_map/return/all_to_all | solution.py:232
  146.5 125.5 %collective-permute-start.2 = (bf16[256,512]{1,0:T(8,128)(2,1)S(1)}, bf16[256,512]{1,0:T(8,128)(2,1)}, u32[]{:S(2)}, u32[]{:S(2)}) collective-permute-start(bf16[256,512]{1,0:T(8,128)(2,1)S(1)} %copy-done.1), channel_id=1, source_target_pairs={{0,384},{128,0},{256,128},{384,256},{1,385},{129,1},{257,129},{385... | collective-permute-start | bytes 786440 | tf_op jit(solution)/shard_map/gather_parts/ppermute | solution.py:230
  152.4 119.6 %collective-permute-start.1 = (bf16[256,512]{1,0:T(8,128)(2,1)S(1)}, bf16[256,512]{1,0:T(8,128)(2,1)}, u32[]{:S(2)}, u32[]{:S(2)}) collective-permute-start(bf16[256,512]{1,0:T(8,128)(2,1)S(1)} %copy-done.1), channel_id=1, source_target_pairs={{0,256},{128,384},{256,0},{384,128},{1,257},{129,385},{257,1},{385... | collective-permute-start | bytes 786440 | tf_op jit(solution)/shard_map/gather_parts/ppermute | solution.py:230
  154.3 117.6 %collective-permute-start = (bf16[256,512]{1,0:T(8,128)(2,1)S(1)}, bf16[256,512]{1,0:T(8,128)(2,1)}, u32[]{:S(2)}, u32[]{:S(2)}) collective-permute-start(bf16[256,512]{1,0:T(8,128)(2,1)S(1)} %copy-done.1), channel_id=1, source_target_pairs={{0,128},{128,256},{256,384},{384,0},{1,129},{129,257},{257,385},{3... | collective-permute-start | bytes 786440 | tf_op jit(solution)/shard_map/gather_parts/ppermute | solution.py:230

commit v7 on v6

--- a/solution.py
+++ b/solution.py
@@ -66,20 +66,8 @@
     out_ref[...] = jnp.swapaxes(jnp.stack(pieces), 0, 1)
 
 
-def middle_kernel(
-    own, cols, shares, arrived_ref, kernel_ref, second_ref, back_ref, part_ref, second_out_ref, total_ref, second_total_ref
-):
-    step = pl.program_id(0)
-    last = pl.num_programs(0) - 1
-    seq_share, factor_share = shares
-
-    @pl.when(step == 0)
-    def _():
-        total_ref[...] = jnp.zeros_like(total_ref)
-        second_total_ref[...] = jnp.zeros_like(second_total_ref)
-
+def products(own, cols, arrived_ref, kernel_ref, second_ref, step):
     arrived = jnp.swapaxes(arrived_ref[step], 0, 1)
-    pieces = [None] * arrived.shape[0]
     for q in range(own):
         factor = second_ref[q]
         mixed_in, mixed_up = beside(arrived, own, cols, q)
@@ -87,15 +75,36 @@
         backward = nn(factor, mixed_up)
         points = factor.shape[0]
         scale = kernel_ref[q * points : (q + 1) * points, :].astype(jnp.float32)
-        total_ref[q] += forward * backward
         weighted = (scale * forward).astype(jnp.bfloat16)
         pulled = (scale * backward).astype(jnp.bfloat16)
-        second_total_ref[q] += (nt(pulled, mixed_in) + nt(weighted, mixed_up)) * factor_share
-        for t, values in enumerate((weighted, pulled)):
+        yield q, factor, (mixed_in, mixed_up), (forward, backward), (weighted, pulled)
+
+
+def middle_kernel(own, cols, arrived_ref, kernel_ref, second_ref, back_ref):
+    pieces = [None] * back_ref.shape[2]
+    for q, factor, _, _, scaled in products(own, cols, arrived_ref, kernel_ref, second_ref, pl.program_id(0)):
+        for t, values in enumerate(scaled):
             spread = tn(factor, values).astype(jnp.bfloat16)
             for ci in range(cols):
                 pieces[(t * cols + ci) * own + q] = spread[:, ci * LANES : (ci + 1) * LANES]
     back_ref[0] = jnp.swapaxes(jnp.stack(pieces), 0, 1)
+
+
+def gradients_kernel(
+    own, cols, shares, arrived_ref, kernel_ref, second_ref, part_ref, second_out_ref, total_ref, second_total_ref
+):
+    step = pl.program_id(0)
+    last = pl.num_programs(0) - 1
+    seq_share, factor_share = shares
+
+    @pl.when(step == 0)
+    def _():
+        total_ref[...] = jnp.zeros_like(total_ref)
+        second_total_ref[...] = jnp.zeros_like(second_total_ref)
+
+    for q, _, mixed, parts, scaled in products(own, cols, arrived_ref, kernel_ref, second_ref, 0):
+        total_ref[q] += parts[0] * parts[1]
+        second_total_ref[q] += (nt(scaled[1], mixed[0]) + nt(scaled[0], mixed[1])) * factor_share
 
     @pl.when(step == last)
     def _():
@@ -202,18 +211,31 @@
     with jax.named_scope("send"):
         arrived = lax.all_to_all(mixed, ("dp", "seq"), split_axis=0, concat_axis=0, tiled=True)
     quarter = lax.dynamic_slice_in_dim(kernel, lax.axis_index("dp") * share, share, 1)
+    held = (arrived.reshape(ranks, members, rows, LANES), quarter, second_factor)
     with jax.named_scope("middle"):
-        back, part, second_part = pl.pallas_call(
-            lambda *refs: middle_kernel(own, cols, (seq_share, factor_share), *refs),
-            out_shape=(
-                pltpu.HBM((ranks, members, rows, LANES), jnp.bfloat16),
-                pltpu.HBM((own * points, share), jnp.bfloat16),
-                pltpu.HBM((points, own * members), jnp.bfloat16),
-            ),
+        back = pl.pallas_call(
+            lambda *refs: middle_kernel(own, cols, *refs),
+            out_shape=pltpu.HBM((ranks, members, rows, LANES), jnp.bfloat16),
             grid=(ranks,),
             in_specs=[vmem, vmem, vmem],
+            out_specs=pl.BlockSpec((1, members, rows, LANES), lambda s: (s, 0, 0, 0)),
+            compiler_params=params,
+            name="middle",
+        )(*held)
+    with jax.named_scope("gradients"):
+        part, second_part = pl.pallas_call(
+            lambda *refs: gradients_kernel(own, cols, (seq_share, factor_share), *refs),
+            out_shape=(
+                jax.ShapeDtypeStruct((own * points, share), jnp.bfloat16),
+                jax.ShapeDtypeStruct((points, own * members), jnp.bfloat16),
+            ),
+            grid=(ranks,),
+            in_specs=[
+                pl.BlockSpec((1, members, rows, LANES), lambda s: (s, 0, 0, 0)),
+                pl.BlockSpec((own * points, share), lambda s: (0, 0)),
+                pl.BlockSpec((own, points, members), lambda s: (0, 0, 0)),
+            ],
             out_specs=(
-                pl.BlockSpec((1, members, rows, LANES), lambda s: (s, 0, 0, 0)),
                 pl.BlockSpec((own * points, share), lambda s: (0, 0)),
                 pl.BlockSpec((points, own * members), lambda s: (0, 0)),
             ),
@@ -221,11 +243,13 @@
                 pltpu.VMEM((own, points, share), jnp.float32),
                 pltpu.VMEM((own, points, members), jnp.float32),
             ],
-            compiler_params=params,
-            name="middle",
-        )(arrived.reshape(ranks, members, rows, LANES), quarter, second_factor)
+            compiler_params=pltpu.CompilerParams(
+                dimension_semantics=("arbitrary",), vmem_limit_bytes=16 * 1024 * 1024
+            ),
+            name="gradients",
+        )(in_hbm(held[0]), *held[1:])
     with jax.named_scope("gather_parts"):
-        pieces = [part]
+        pieces = [in_hbm(part)]
         for r in range(1, ranks):
             pieces.append(lax.ppermute(part, "dp", [(i, (i + r) % ranks) for i in range(ranks)]))
     with jax.named_scope("return"):

time: 277 us -> 276 us (level)
  waiting for transfers between devices: 192 us -> 187 us
  Pallas kernels: 15.8 us -> 20.2 us
    all_to_all x1, waiting for transfers between devices: 90.8 us -> 86 us  [shards(): lax.all_to_all(back.reshape(ranks * members, rows, LANES), ('dp', 'seq'),...]
    pallas_call x1 -> x2, Pallas kernels: 4.48 us -> 8.91 us  [the longest x1 4.87 us: shards(): pl.pallas_call(lambda *refs: gradients_kernel(own, cols, (seq_share, fact...]
  transfers between devices with their start and end apart: 5 -> 5, of which waited for: 2 -> 2; matrix products, arithmetic and copies ran while one was open for 0% -> 0% of each run, Pallas kernels for 1% -> 3%
where the time goes in v7:
time: 276 us; the launch traced here: 274 us
  waiting for transfers between devices  187 us (68%)
  starting transfers between devices  45.3 us (16%)
  blocking collectives  20.7 us (8%)
  Pallas kernels  20.2 us (7%)
    all_to_all x1, waiting for transfers between devices, shards(): lax.all_to_all(mixed, ('dp', 'seq'), split_axis=0, concat_axis=0, tiled=T...  101 us
    all_to_all x1, waiting for transfers between devices, shards(): lax.all_to_all(back.reshape(ranks * members, rows, LANES), ('dp', 'seq'),...  86 us
    all_to_all x1, starting transfers between devices, shards(): lax.all_to_all(mixed, ('dp', 'seq'), split_axis=0, concat_axis=0, tiled=T...  24.3 us
    all_gather x1, blocking collectives, shards(): gathered = lax.all_gather(factor_parts, 'dp')  20.7 us
    all_to_all x1, starting transfers between devices, shards(): lax.all_to_all(back.reshape(ranks * members, rows, LANES), ('dp', 'seq'),...  11 us
    ppermute x3, starting transfers between devices, shards(): lax.ppermute(part, 'dp', [(i, (i + r) % ranks) for i in range(ranks)])  10 us
  transfers between devices with their start and end apart: 5, of which 2 were waited for; matrix products, arithmetic and copies ran while one was open for 0% of the time, Pallas kernels for 3%

profile of v7, /device:TPU:1, one launch (start us, length us, event | category | flops | bytes accessed | tf_op | source)
XLA Modules:
  0.0 274.1 jit_solution(6824361577550545794)
XLA Ops:
  0.6 0.0 copy-start
  0.6 4.7 %mix.1 = bf16[512,16,128]{2,1,0:T(8,128)(2,1)} custom-call(bf16[1,256,256]{2,1,0:T(8,128)(2,1)} %refs_0_.1, bf16[1,256,2048]{2,1,0:T(8,128)(2,1)} %refs_2_.7, bf16[1,256,2048]{2,1,0:T(8,128)(2,1)} %refs_3_.1), custom_call_target="tpu_custom_call" | custom-call | tf_op jit(solution)/shard_map/mix/mix/pallas_call | solution.py:197
  5.4 0.0 copy-start.2
  5.4 24.3 %all-to-all-start = ((bf16[512,16,128]{2,1,0:T(8,128)(2,1)}), bf16[512,16,128]{2,1,0:T(8,128)(2,1)S(1)}, u32[]{:S(2)}, u32[]{:S(2)}) async-start(bf16[512,16,128]{2,1,0:T(8,128)(2,1)} %mix.1), calls=%async_computation | async-start | bytes 4194304 | tf_op jit(solution)/shard_map/send/all_to_all | solution.py:212
  29.7 0.0 copy-done
  29.7 101.1 %all-to-all-done = bf16[512,16,128]{2,1,0:T(8,128)(2,1)S(1)} async-done(((bf16[512,16,128]{2,1,0:T(8,128)(2,1)}), bf16[512,16,128]{2,1,0:T(8,128)(2,1)S(1)}, u32[]{:S(2)}, u32[]{:S(2)}) %all-to-all-start) | async-done | bytes 2097184 | tf_op jit(solution)/shard_map/send/all_to_all | solution.py:212
  130.8 0.0 copy-start.1
  130.8 0.0 copy-done.2
  130.8 4.0 %middle.1 = bf16[4,128,16,128]{3,2,1,0:T(8,128)(2,1)} custom-call(bf16[4,128,16,128]{3,2,1,0:T(8,128)(2,1)S(1)} %bitcast.5, bf16[256,512]{1,0:T(8,128)(2,1)S(1)} %constant_dynamic-slice_fusion.refs_1_, bf16[2,128,128]{2,1,0:T(8,128)(2,1)S(1)} %copy-done.2), custom_call_target="tpu_custom_call" | custom-call | tf_op jit(solution)/shard_map/middle/middle/pallas_call | solution.py:216
  134.9 0.0 copy-done.1
  134.9 11.0 %all-to-all-start.1 = ((bf16[512,16,128]{2,1,0:T(8,128)(2,1)}), bf16[512,16,128]{2,1,0:T(8,128)(2,1)S(1)}, u32[]{:S(2)}, u32[]{:S(2)}) async-start(bf16[512,16,128]{2,1,0:T(8,128)(2,1)} %bitcast.9), calls=%async_computation.1 | async-start | bytes 4194304 | tf_op jit(solution)/shard_map/return/all_to_all | solution.py:256
  145.9 4.9 %gradients.1 = (bf16[256,512]{1,0:T(8,128)(2,1)}, bf16[128,256]{1,0:T(8,128)(2,1)S(1)}) custom-call(bf16[4,128,16,128]{3,2,1,0:T(8,128)(2,1)} %bitcast.6, bf16[256,512]{1,0:T(8,128)(2,1)S(1)} %constant_dynamic-slice_fusion.refs_1_, bf16[2,128,128]{2,1,0:T(8,128)(2,1)S(1)} %copy-done.2), custom_call_target="tpu_custom_call" | custom-call | tf_op jit(solution)/shard_map/gradients/gradients/pallas_call | solution.py:226
  150.8 5.9 %collective-permute-start.2 = (bf16[256,512]{1,0:T(8,128)(2,1)}, bf16[256,512]{1,0:T(8,128)(2,1)S(1)}, u32[]{:S(2)}, u32[]{:S(2)}) collective-permute-start(bf16[256,512]{1,0:T(8,128)(2,1)} %get-tuple-element.9.refs_1_), channel_id=1, source_target_pairs={{0,384},{128,0},{256,128},{384,256},{1,385},{129,1},{257,129},{385... | collective-permute-start | bytes 786440 | tf_op jit(solution)/shard_map/gather_parts/ppermute | solution.py:254
  156.6 1.9 collective-permute-start.1
  158.6 2.2 collective-permute-start
  160.8 86.0 %all-to-all-done.1 = bf16[512,16,128]{2,1,0:T(8,128)(2,1)S(1)} async-done(((bf16[512,16,128]{2,1,0:T(8,128)(2,1)}), bf16[512,16,128]{2,1,0:T(8,128)(2,1)S(1)}, u32[]{:S(2)}, u32[]{:S(2)}) %all-to-all-start.1) | async-done | bytes 2097184 | tf_op jit(solution)/shard_map/return/all_to_all | solution.py:256
  246.8 3.8 %final.1 = bf16[384,256]{1,0:T(8,128)(2,1)S(1)} custom-call(bf16[4,128,16,128]{3,2,1,0:T(8,128)(2,1)S(1)} %bitcast.7, bf16[128,256]{1,0:T(8,128)(2,1)S(1)} %get-tuple-element.8.refs_1_, bf16[1,256,2048]{2,1,0:T(8,128)(2,1)} %refs_2_.7, bf16[1,256,2048]{2,1,0:T(8,128)(2,1)} %refs_3_.1), custom_call_target="tpu_custom_call" | custom-call | tf_op jit(solution)/shard_map/final/final/pallas_call | solution.py:260
  250.6 20.7 %all-gather = bf16[1536,256]{1,0:T(8,128)(2,1)S(1)} all-gather(bf16[384,256]{1,0:T(8,128)(2,1)S(1)} %final.1), channel_id=2, replica_groups=mesh['dp'=4,'seq'=128] {'dp'}, dimensions={0}, use_global_device_ids=true | all-gather | bytes 983040 | tf_op jit(solution)/shard_map/sum/all_gather | solution.py:276
  271.4 0.0 collective-permute-done.2.refs_4_
  271.4 0.0 collective-permute-done.1.refs_3_
  271.4 0.0 collective-permute-done.refs_2_
  271.4 2.7 join.1
  (1 shorter events, 0.0 us)
Async XLA Ops:
  0.6 29.1 %copy-start = (bf16[256,2048]{1,0:T(8,128)(2,1)S(1)}, bf16[256,2048]{1,0:T(8,128)(2,1)}, u32[]{:S(2)}) copy-start(bf16[256,2048]{1,0:T(8,128)(2,1)} %param.7) | copy-start | bytes 3145732
  5.4 125.4 %copy-start.2 = (bf16[2,128,128]{2,1,0:T(8,128)(2,1)S(1)}, bf16[2,128,128]{2,1,0:T(8,128)(2,1)}, u32[]{:S(2)}) copy-start(bf16[2,128,128]{2,1,0:T(8,128)(2,1)} %refs_2_.6) | copy-start | bytes 196612
  5.4 125.4 %all-to-all-start = ((bf16[512,16,128]{2,1,0:T(8,128)(2,1)}), bf16[512,16,128]{2,1,0:T(8,128)(2,1)S(1)}, u32[]{:S(2)}, u32[]{:S(2)}) async-start(bf16[512,16,128]{2,1,0:T(8,128)(2,1)} %mix.1), calls=%async_computation | async-start | bytes 4194304 | tf_op jit(solution)/shard_map/send/all_to_all | solution.py:212
  130.8 4.0 %copy-start.1 = (bf16[512,16,128]{2,1,0:T(8,128)(2,1)}, bf16[512,16,128]{2,1,0:T(8,128)(2,1)S(1)}, u32[]{:S(2)}) copy-start(bf16[512,16,128]{2,1,0:T(8,128)(2,1)S(1)} %all-to-all-done) | copy-start | bytes 6291460
  134.9 111.9 %all-to-all-start.1 = ((bf16[512,16,128]{2,1,0:T(8,128)(2,1)}), bf16[512,16,128]{2,1,0:T(8,128)(2,1)S(1)}, u32[]{:S(2)}, u32[]{:S(2)}) async-start(bf16[512,16,128]{2,1,0:T(8,128)(2,1)} %bitcast.9), calls=%async_computation.1 | async-start | bytes 4194304 | tf_op jit(solution)/shard_map/return/all_to_all | solution.py:256
  150.8 120.6 %collective-permute-start.2 = (bf16[256,512]{1,0:T(8,128)(2,1)}, bf16[256,512]{1,0:T(8,128)(2,1)S(1)}, u32[]{:S(2)}, u32[]{:S(2)}) collective-permute-start(bf16[256,512]{1,0:T(8,128)(2,1)} %get-tuple-element.9.refs_1_), channel_id=1, source_target_pairs={{0,384},{128,0},{256,128},{384,256},{1,385},{129,1},{257,129},{385... | collective-permute-start | bytes 786440 | tf_op jit(solution)/shard_map/gather_parts/ppermute | solution.py:254
  156.6 114.7 %collective-permute-start.1 = (bf16[256,512]{1,0:T(8,128)(2,1)}, bf16[256,512]{1,0:T(8,128)(2,1)}, u32[]{:S(2)}, u32[]{:S(2)}) collective-permute-start(bf16[256,512]{1,0:T(8,128)(2,1)} %get-tuple-element.9.refs_1_), channel_id=1, source_target_pairs={{0,256},{128,384},{256,0},{384,128},{1,257},{129,385},{257,1},{385... | collective-permute-start | bytes 786440 | tf_op jit(solution)/shard_map/gather_parts/ppermute | solution.py:254
  158.6 112.8 %collective-permute-start = (bf16[256,512]{1,0:T(8,128)(2,1)}, bf16[256,512]{1,0:T(8,128)(2,1)}, u32[]{:S(2)}, u32[]{:S(2)}) collective-permute-start(bf16[256,512]{1,0:T(8,128)(2,1)} %get-tuple-element.9.refs_1_), channel_id=1, source_target_pairs={{0,128},{128,256},{256,384},{384,0},{1,129},{129,257},{257,385},{3... | collective-permute-start | bytes 786440 | tf_op jit(solution)/shard_map/gather_parts/ppermute | solution.py:254

commit v8 on v7

--- a/solution.py
+++ b/solution.py
@@ -35,18 +35,23 @@
     ]
 
 
-def mix_kernel(own, cols, ranks, first_ref, tokens_ref, cotangent_ref, out_ref, factor_ref, held_ref, sems):
+def mix_kernel(
+    own, cols, ranks, first_ref, tokens_ref, cotangent_ref, out_ref, raw_ref, factor_ref, held_ref, first_sem, sems
+):
     groups = out_ref.shape[0]
     step = pl.program_id(0)
     sources = (tokens_ref, cotangent_ref)
 
     @pl.when(step == 0)
     def _():
+        first = pltpu.make_async_copy(first_ref.at[0], raw_ref, first_sem)
+        first.start()
         for k in range(ranks):
             for copy in loads(sources, held_ref, sems, cols * LANES, k):
                 copy.start()
+        first.wait()
         for h in range(factor_ref.shape[0]):
-            factor_ref[h] = first_ref[0, :, h * LANES : (h + 1) * LANES].astype(jnp.float32)
+            factor_ref[h] = raw_ref[:, h * LANES : (h + 1) * LANES].astype(jnp.float32)
 
     for copy in loads(sources, held_ref, sems, cols * LANES, step):
         copy.wait()
@@ -198,11 +203,13 @@
             lambda *refs: mix_kernel(own, cols, ranks, *refs),
             out_shape=pltpu.HBM((ranks * members, rows, LANES), jnp.bfloat16),
             grid=(ranks,),
-            in_specs=[pl.BlockSpec((1, local_rows, local_rows), lambda k: (0, 0, 0)), whole, whole],
+            in_specs=[whole, whole, whole],
             out_specs=pl.BlockSpec((members, rows, LANES), lambda k: (k, 0, 0)),
             scratch_shapes=[
+                pltpu.VMEM((local_rows, local_rows), jnp.bfloat16),
                 pltpu.VMEM((local_rows // LANES, local_rows, LANES), jnp.float32),
                 pltpu.VMEM((2, ranks, local_rows, share), jnp.bfloat16),
+                pltpu.SemaphoreType.DMA(()),
                 pltpu.SemaphoreType.DMA((2, ranks)),
             ],
             compiler_params=params,

time: 276 us -> 276 us (level)
  no operation moved by 1% of the time
where the time goes in v8:
time: 276 us; the launch traced here: 274 us
  waiting for transfers between devices  187 us (68%)
  starting transfers between devices  45.3 us (16%)
  blocking collectives  20.7 us (8%)
  Pallas kernels  19.7 us (7%)
    all_to_all x1, waiting for transfers between devices, shards(): lax.all_to_all(mixed, ('dp', 'seq'), split_axis=0, concat_axis=0, tiled=T...  101 us
    all_to_all x1, waiting for transfers between devices, shards(): lax.all_to_all(back.reshape(ranks * members, rows, LANES), ('dp', 'seq'),...  86 us
    all_to_all x1, starting transfers between devices, shards(): lax.all_to_all(mixed, ('dp', 'seq'), split_axis=0, concat_axis=0, tiled=T...  24.3 us
    all_gather x1, blocking collectives, shards(): gathered = lax.all_gather(factor_parts, 'dp')  20.7 us
    all_to_all x1, starting transfers between devices, shards(): lax.all_to_all(back.reshape(ranks * members, rows, LANES), ('dp', 'seq'),...  11 us
    ppermute x3, starting transfers between devices, shards(): lax.ppermute(part, 'dp', [(i, (i + r) % ranks) for i in range(ranks)])  10 us
  transfers between devices with their start and end apart: 5, of which 2 were waited for; matrix products, arithmetic and copies ran while one was open for 0% of the time, Pallas kernels for 3%

profile of v8, /device:TPU:1, one launch (start us, length us, event | category | flops | bytes accessed | tf_op | source)
XLA Modules:
  0.0 273.6 jit_solution(18198678415625672181)
XLA Ops:
  0.6 0.0 copy-start
  0.6 4.3 %mix.1 = bf16[512,16,128]{2,1,0:T(8,128)(2,1)} custom-call(bf16[1,256,256]{2,1,0:T(8,128)(2,1)} %refs_0_.1, bf16[1,256,2048]{2,1,0:T(8,128)(2,1)} %refs_2_.7, bf16[1,256,2048]{2,1,0:T(8,128)(2,1)} %refs_3_.1), custom_call_target="tpu_custom_call" | custom-call | tf_op jit(solution)/shard_map/mix/mix/pallas_call | solution.py:202
  4.9 0.0 copy-start.2
  4.9 24.3 %all-to-all-start = ((bf16[512,16,128]{2,1,0:T(8,128)(2,1)}), bf16[512,16,128]{2,1,0:T(8,128)(2,1)S(1)}, u32[]{:S(2)}, u32[]{:S(2)}) async-start(bf16[512,16,128]{2,1,0:T(8,128)(2,1)} %mix.1), calls=%async_computation | async-start | bytes 4194304 | tf_op jit(solution)/shard_map/send/all_to_all | solution.py:219
  29.3 0.0 copy-done
  29.3 101.1 %all-to-all-done = bf16[512,16,128]{2,1,0:T(8,128)(2,1)S(1)} async-done(((bf16[512,16,128]{2,1,0:T(8,128)(2,1)}), bf16[512,16,128]{2,1,0:T(8,128)(2,1)S(1)}, u32[]{:S(2)}, u32[]{:S(2)}) %all-to-all-start) | async-done | bytes 2097184 | tf_op jit(solution)/shard_map/send/all_to_all | solution.py:219
  130.4 0.0 copy-start.1
  130.4 0.0 copy-done.2
  130.4 4.0 %middle.1 = bf16[4,128,16,128]{3,2,1,0:T(8,128)(2,1)} custom-call(bf16[4,128,16,128]{3,2,1,0:T(8,128)(2,1)S(1)} %bitcast.5, bf16[256,512]{1,0:T(8,128)(2,1)S(1)} %constant_dynamic-slice_fusion.refs_1_, bf16[2,128,128]{2,1,0:T(8,128)(2,1)S(1)} %copy-done.2), custom_call_target="tpu_custom_call" | custom-call | tf_op jit(solution)/shard_map/middle/middle/pallas_call | solution.py:223
  134.4 0.0 copy-done.1
  134.4 11.0 %all-to-all-start.1 = ((bf16[512,16,128]{2,1,0:T(8,128)(2,1)}), bf16[512,16,128]{2,1,0:T(8,128)(2,1)S(1)}, u32[]{:S(2)}, u32[]{:S(2)}) async-start(bf16[512,16,128]{2,1,0:T(8,128)(2,1)} %bitcast.9), calls=%async_computation.1 | async-start | bytes 4194304 | tf_op jit(solution)/shard_map/return/all_to_all | solution.py:263
  145.4 4.9 %gradients.1 = (bf16[256,512]{1,0:T(8,128)(2,1)}, bf16[128,256]{1,0:T(8,128)(2,1)S(1)}) custom-call(bf16[4,128,16,128]{3,2,1,0:T(8,128)(2,1)} %bitcast.6, bf16[256,512]{1,0:T(8,128)(2,1)S(1)} %constant_dynamic-slice_fusion.refs_1_, bf16[2,128,128]{2,1,0:T(8,128)(2,1)S(1)} %copy-done.2), custom_call_target="tpu_custom_call" | custom-call | tf_op jit(solution)/shard_map/gradients/gradients/pallas_call | solution.py:233
  150.3 5.9 %collective-permute-start.2 = (bf16[256,512]{1,0:T(8,128)(2,1)}, bf16[256,512]{1,0:T(8,128)(2,1)S(1)}, u32[]{:S(2)}, u32[]{:S(2)}) collective-permute-start(bf16[256,512]{1,0:T(8,128)(2,1)} %get-tuple-element.9.refs_1_), channel_id=1, source_target_pairs={{0,384},{128,0},{256,128},{384,256},{1,385},{129,1},{257,129},{385... | collective-permute-start | bytes 786440 | tf_op jit(solution)/shard_map/gather_parts/ppermute | solution.py:261
  156.2 1.9 collective-permute-start.1
  158.1 2.2 collective-permute-start
  160.3 86.0 %all-to-all-done.1 = bf16[512,16,128]{2,1,0:T(8,128)(2,1)S(1)} async-done(((bf16[512,16,128]{2,1,0:T(8,128)(2,1)}), bf16[512,16,128]{2,1,0:T(8,128)(2,1)S(1)}, u32[]{:S(2)}, u32[]{:S(2)}) %all-to-all-start.1) | async-done | bytes 2097184 | tf_op jit(solution)/shard_map/return/all_to_all | solution.py:263
  246.3 3.8 %final.1 = bf16[384,256]{1,0:T(8,128)(2,1)S(1)} custom-call(bf16[4,128,16,128]{3,2,1,0:T(8,128)(2,1)S(1)} %bitcast.7, bf16[128,256]{1,0:T(8,128)(2,1)S(1)} %get-tuple-element.8.refs_1_, bf16[1,256,2048]{2,1,0:T(8,128)(2,1)} %refs_2_.7, bf16[1,256,2048]{2,1,0:T(8,128)(2,1)} %refs_3_.1), custom_call_target="tpu_custom_call" | custom-call | tf_op jit(solution)/shard_map/final/final/pallas_call | solution.py:267
  250.1 20.7 %all-gather = bf16[1536,256]{1,0:T(8,128)(2,1)S(1)} all-gather(bf16[384,256]{1,0:T(8,128)(2,1)S(1)} %final.1), channel_id=2, replica_groups=mesh['dp'=4,'seq'=128] {'dp'}, dimensions={0}, use_global_device_ids=true | all-gather | bytes 983040 | tf_op jit(solution)/shard_map/sum/all_gather | solution.py:283
  270.9 0.0 collective-permute-done.2.refs_4_
  270.9 0.0 collective-permute-done.1.refs_3_
  270.9 0.0 collective-permute-done.refs_2_
  270.9 2.7 join.1
  (1 shorter events, 0.0 us)
Async XLA Ops:
  0.6 28.6 %copy-start = (bf16[256,2048]{1,0:T(8,128)(2,1)S(1)}, bf16[256,2048]{1,0:T(8,128)(2,1)}, u32[]{:S(2)}) copy-start(bf16[256,2048]{1,0:T(8,128)(2,1)} %param.7) | copy-start | bytes 3145732
  4.9 125.4 %copy-start.2 = (bf16[2,128,128]{2,1,0:T(8,128)(2,1)S(1)}, bf16[2,128,128]{2,1,0:T(8,128)(2,1)}, u32[]{:S(2)}) copy-start(bf16[2,128,128]{2,1,0:T(8,128)(2,1)} %refs_2_.6) | copy-start | bytes 196612
  4.9 125.4 %all-to-all-start = ((bf16[512,16,128]{2,1,0:T(8,128)(2,1)}), bf16[512,16,128]{2,1,0:T(8,128)(2,1)S(1)}, u32[]{:S(2)}, u32[]{:S(2)}) async-start(bf16[512,16,128]{2,1,0:T(8,128)(2,1)} %mix.1), calls=%async_computation | async-start | bytes 4194304 | tf_op jit(solution)/shard_map/send/all_to_all | solution.py:219
  130.4 4.0 %copy-start.1 = (bf16[512,16,128]{2,1,0:T(8,128)(2,1)}, bf16[512,16,128]{2,1,0:T(8,128)(2,1)S(1)}, u32[]{:S(2)}) copy-start(bf16[512,16,128]{2,1,0:T(8,128)(2,1)S(1)} %all-to-all-done) | copy-start | bytes 6291460
  134.4 111.9 %all-to-all-start.1 = ((bf16[512,16,128]{2,1,0:T(8,128)(2,1)}), bf16[512,16,128]{2,1,0:T(8,128)(2,1)S(1)}, u32[]{:S(2)}, u32[]{:S(2)}) async-start(bf16[512,16,128]{2,1,0:T(8,128)(2,1)} %bitcast.9), calls=%async_computation.1 | async-start | bytes 4194304 | tf_op jit(solution)/shard_map/return/all_to_all | solution.py:263
  150.3 120.6 %collective-permute-start.2 = (bf16[256,512]{1,0:T(8,128)(2,1)}, bf16[256,512]{1,0:T(8,128)(2,1)S(1)}, u32[]{:S(2)}, u32[]{:S(2)}) collective-permute-start(bf16[256,512]{1,0:T(8,128)(2,1)} %get-tuple-element.9.refs_1_), channel_id=1, source_target_pairs={{0,384},{128,0},{256,128},{384,256},{1,385},{129,1},{257,129},{385... | collective-permute-start | bytes 786440 | tf_op jit(solution)/shard_map/gather_parts/ppermute | solution.py:261
  156.2 114.7 %collective-permute-start.1 = (bf16[256,512]{1,0:T(8,128)(2,1)}, bf16[256,512]{1,0:T(8,128)(2,1)}, u32[]{:S(2)}, u32[]{:S(2)}) collective-permute-start(bf16[256,512]{1,0:T(8,128)(2,1)} %get-tuple-element.9.refs_1_), channel_id=1, source_target_pairs={{0,256},{128,384},{256,0},{384,128},{1,257},{129,385},{257,1},{385... | collective-permute-start | bytes 786440 | tf_op jit(solution)/shard_map/gather_parts/ppermute | solution.py:261
  158.1 112.8 %collective-permute-start = (bf16[256,512]{1,0:T(8,128)(2,1)}, bf16[256,512]{1,0:T(8,128)(2,1)}, u32[]{:S(2)}, u32[]{:S(2)}) collective-permute-start(bf16[256,512]{1,0:T(8,128)(2,1)} %get-tuple-element.9.refs_1_), channel_id=1, source_target_pairs={{0,128},{128,256},{256,384},{384,0},{1,129},{129,257},{257,385},{3... | collective-permute-start | bytes 786440 | tf_op jit(solution)/shard_map/gather_parts/ppermute | solution.py:261
